TPU v7x, 256 devices: a whole 4x4x8 slice. The times are simulated.
256 devices in a mesh: ctx: 32 (over y, x, core), mp: 8 (over z).
Axes of the slice: x: 4, y: 4, z: 8, core: 2. Of those that a mesh axis runs over, the one named last changes fastest.
Arguments:
- tokens: bfloat16 [8192, 4096], P(('ctx', 'mp')), may hold values from -6 to 6
- branch: bfloat16 [8192, 4096], P('ctx', 'mp'), may hold values from -4 to 4
- out_grad: bfloat16 [8192, 4096], P(('ctx', 'mp')), may hold values from -24 to 24
- w_in: bfloat16 [4096, 4096], P(None, 'mp'), may hold values from -0.09375 to 0.09375
- conv_w: bfloat16 [4, 4096], P(None, 'mp'), may hold values from -3 to 3
- gate_a_w: bfloat16 [16, 256, 256], P('mp'), may hold values from -0.375 to 0.375
- gate_a_b: float32 [4096], P('mp'), may hold values from -4 to 4
- gate_i_w: bfloat16 [16, 256, 256], P('mp'), may hold values from -0.375 to 0.375
- gate_i_b: float32 [4096], P('mp'), may hold values from -4 to 4
- decay_param: float32 [4096], P('mp')
- w_out: bfloat16 [4096, 4096], P('mp'), may hold values from -0.09375 to 0.09375
- state_init: float32 [4096], P('mp'), may hold values from -5 to 5
- conv_history: bfloat16 [3, 4096], P(None, 'mp'), may hold values from -5 to 5
Outputs:
- tokens_grad: bfloat16 [8192, 4096], P(('ctx', 'mp'))
- branch_grad: bfloat16 [8192, 4096], P('ctx', 'mp')
- w_in_grad: float32 [4096, 4096], P('ctx', 'mp')
- w_out_grad: float32 [4096, 4096], P('mp', 'ctx')
- conv_w_grad: float32 [4, 4096], P(None, 'mp')
- gate_a_w_grad: float32 [16, 256, 256], P('mp')
- gate_a_b_grad: float32 [4096], P('mp')
- gate_i_w_grad: float32 [16, 256, 256], P('mp')
- gate_i_b_grad: float32 [4096], P('mp')
- decay_grad: float32 [4096], P('mp')
All inputs are finite; a program needn't handle non-finite values.
Results may differ from a plain program's by a relative error of at most 0.02.
Values may be sent and summed in bfloat16 or wider, within the bound.
A program may use at most 128 MiB of HBM per device.

v0:
```python
import jax
import jax.numpy as jnp
from jax import lax
from jax.sharding import PartitionSpec as P


def sent_together(arrays, axis, dim, along):
    ends, at = ([], 0)
    for a in arrays[:-1]:
        at += a.shape[along]
        ends.append(at)
    both = jnp.concatenate(arrays, axis=along)
    return tuple(jnp.split(lax.all_gather(both, axis, axis=dim, tiled=True), ends, axis=along))


def from_behind(block, axis, distance):
    devices = range(lax.axis_size(axis))
    route = [(i - distance, i) for i in devices if i - distance in devices]
    return lax.ppermute(block, axis, route)


def copy_for_each(value, axis):
    copies = jnp.broadcast_to(value, (lax.axis_size(axis), *value.shape))
    return lax.all_to_all(copies, axis, split_axis=0, concat_axis=0, tiled=True)


def gathered_once(value, axis):
    leaves = jax.tree.leaves(value)
    turns = sorted(range(len(leaves)), key=lambda k: -leaves[k].size)
    width = (1, *leaves[turns[0]].shape)[-1]
    lines = [
        jnp.pad(leaves[k].reshape(-1), (0, -leaves[k].size % width)).reshape(-1, width)
        for k in turns
    ]
    both, at, found = (copy_for_each(jnp.concatenate(lines), axis), 0, {})
    for k, line in zip(turns, lines):
        piece = both[:, at : at + len(line)].reshape(len(both), -1)
        found[k] = piece[:, : leaves[k].size].reshape(-1, *leaves[k].shape)
        at += len(line)
    numbers = iter(range(len(leaves)))
    return jax.tree.map(lambda _: found[next(numbers)], value)


def joined_by_halves(pieces, combine):
    while len(jax.tree.leaves(pieces)[0]) > 1:
        pieces = jax.vmap(combine)(
            *(jax.tree.map(lambda part: part[side::2], pieces) for side in (0, 1))
        )
    return jax.tree.map(lambda part: part[0], pieces)


def entering(value, axis, combine, identity, reverse):
    peers, here = (lax.axis_size(axis), lax.axis_index(axis))
    passed = jnp.arange(peers) > here if reverse else jnp.arange(peers) < here

    def kept(part, zero, own):
        part = jnp.where(
            passed.reshape(-1, *(1 for _ in own.shape)), part, jnp.asarray(zero, own.dtype)
        )
        return part[::-1] if reverse else part

    pieces = gathered_once(value, axis)
    return joined_by_halves(jax.tree.map(kept, pieces, identity, value), combine)


def cut_along(value, dim, peers):
    lengths = value.shape
    parts = value.reshape(*lengths[:dim], peers, lengths[dim] // peers, *lengths[dim + 1 :])
    return jnp.moveaxis(parts, dim, 0)


def sum_at_owner(value, axis, dim):
    peers = lax.axis_size(axis)
    parts = lax.all_to_all(cut_along(value, dim, peers), axis, 0, 0, tiled=True)
    return jnp.sum(parts.astype(jnp.float32), axis=0)


def one_scatter(arrays, axis, dims):
    peers = lax.axis_size(axis)
    parts = [cut_along(a, dim, peers) for a, dim in zip(arrays, dims)]
    lines = jnp.concatenate([b.reshape(peers, -1) for b in parts], axis=1)
    rows = max(16, -(-lines.shape[1] // 1024) * 8)
    lines = jnp.pad(lines, ((0, 0), (0, rows * 128 - lines.shape[1]))).reshape(-1, 128)
    ravelled, at, gathered = (lax.psum_scatter(lines, axis, tiled=True).reshape(-1), 0, [])
    for b in parts:
        part = b[0]
        gathered.append(ravelled[at : at + part.size].reshape(part.shape))
        at += part.size
    return tuple(gathered)


def linear_pair(earlier, later):
    return (earlier[0] * later[0], later[0] * earlier[1] + later[1])


def matmul_tn(left, right):
    return lax.dot_general(
        left, right, (((0,), (0,)), ((), ())), preferred_element_type=jnp.float32
    )


def matmul_nt(left, right):
    return lax.dot_general(
        left, right, (((1,), (1,)), ((), ())), preferred_element_type=jnp.float32
    )


def shards(
    tokens,
    branch,
    out_grad,
    w_in,
    conv_w,
    gate_a_w,
    gate_a_b,
    gate_i_w,
    gate_i_b,
    decay_param,
    w_out,
    state_init,
    conv_history,
):
    token_block, grad_block = sent_together((tokens, out_grad), "mp", 0, 1)
    length = token_block.shape[0]
    channels = w_in.shape[1]
    blocks = gate_a_w.shape[0]
    block = gate_a_w.shape[1]
    taps = conv_w.shape[0]
    at_start = lax.axis_index("ctx") == 0
    projected = jnp.dot(token_block, w_in, preferred_element_type=jnp.float32).astype(jnp.bfloat16)
    earlier_rows = from_behind(projected[length - (taps - 1) :], "ctx", 1)
    earlier_rows = jnp.where(at_start, conv_history, earlier_rows)
    extended = jnp.concatenate([earlier_rows, projected], 0).astype(jnp.float32)
    kernel = conv_w.astype(jnp.float32)
    conv_sum = jnp.zeros((length, channels), jnp.float32)
    for shift_by in range(taps):
        conv_sum = (
            conv_sum
            + kernel[shift_by] * extended[taps - 1 - shift_by : taps - 1 - shift_by + length]
        )
    conv_out = conv_sum.astype(jnp.bfloat16)
    conv_wide = conv_out.astype(jnp.float32)
    conv_blocks = conv_out.reshape(length, blocks, block)
    recur_gate = jax.nn.sigmoid(
        jnp.einsum(
            "thb,hbc->thc", conv_blocks, gate_a_w, preferred_element_type=jnp.float32
        ).reshape(length, channels)
        + gate_a_b
    )
    input_gate = jax.nn.sigmoid(
        jnp.einsum(
            "thb,hbc->thc", conv_blocks, gate_i_w, preferred_element_type=jnp.float32
        ).reshape(length, channels)
        + gate_i_b
    )
    softrate = jax.nn.softplus(-decay_param)
    log_decay = -8.0 * recur_gate * softrate
    decay = jnp.exp(log_decay)
    remain = -jnp.expm1(2.0 * log_decay)
    scaler = jnp.sqrt(remain)
    driven = scaler * input_gate * conv_wide
    decay_cum, state_local = lax.associative_scan(linear_pair, (decay, driven), axis=0)
    ones_row = jnp.ones((channels,), jnp.float32)
    zeros_row = jnp.zeros((channels,), jnp.float32)
    prior_decay, prior_state = entering(
        (decay_cum[-1], state_local[-1]), "ctx", linear_pair, (ones_row, zeros_row), False
    )
    state_in = prior_state + prior_decay * state_init
    states = state_local + decay_cum * state_in
    branch_wide = branch.astype(jnp.float32)
    gated_out = (states * branch_wide).astype(jnp.bfloat16)
    grad_gated = matmul_nt(grad_block, w_out)
    branch_grad = (grad_gated * states).astype(jnp.bfloat16)
    state_grad = grad_gated * branch_wide
    flipped_prod, flipped_carry = lax.associative_scan(
        linear_pair, (jnp.flip(decay, 0), jnp.flip(decay * state_grad, 0)), axis=0
    )
    prod_after = jnp.flip(flipped_prod, 0)
    carry_local = jnp.flip(flipped_carry, 0)
    later_prod, carry_in = entering(
        (prod_after[0], carry_local[0]), "ctx", linear_pair, (ones_row, zeros_row), True
    )
    carried = carry_local + prod_after * carry_in
    adjoint = state_grad + jnp.concatenate([carried[1:], carry_in[None]], 0)
    previous = jnp.concatenate([state_in[None], states[:-1]], 0)
    scaler_grad = adjoint * input_gate * conv_wide
    log_grad = adjoint * previous * decay - 2.0 * decay * decay * scaler_grad / jnp.sqrt(
        jnp.maximum(4.0 * remain, 1e-06)
    )
    recur_pre = (log_grad * (-8.0 * softrate) * recur_gate * (1.0 - recur_gate)).astype(
        jnp.bfloat16
    )
    input_pre = (adjoint * scaler * conv_wide * input_gate * (1.0 - input_gate)).astype(
        jnp.bfloat16
    )
    recur_blocks = recur_pre.reshape(length, blocks, block)
    input_blocks = input_pre.reshape(length, blocks, block)
    gate_a_local = jnp.einsum(
        "thb,thc->hbc", conv_blocks, recur_blocks, preferred_element_type=jnp.float32
    )
    gate_i_local = jnp.einsum(
        "thb,thc->hbc", conv_blocks, input_blocks, preferred_element_type=jnp.float32
    )
    bias_a_local = jnp.sum(recur_pre.astype(jnp.float32), 0)
    bias_i_local = jnp.sum(input_pre.astype(jnp.float32), 0)
    rate_local = jnp.sum(log_grad * (-8.0 * recur_gate), 0)
    conv_grad = adjoint * scaler * input_gate
    conv_grad = conv_grad + jnp.einsum(
        "thc,hbc->thb", recur_blocks, gate_a_w, preferred_element_type=jnp.float32
    ).reshape(length, channels)
    conv_grad = conv_grad + jnp.einsum(
        "thc,hbc->thb", input_blocks, gate_i_w, preferred_element_type=jnp.float32
    ).reshape(length, channels)
    later_rows = from_behind(conv_grad[: taps - 1], "ctx", -1)
    padded = jnp.concatenate([conv_grad, later_rows], 0)
    proj_sum = jnp.zeros((length, channels), jnp.float32)
    tap_grads = []
    for shift_by in range(taps):
        proj_sum = proj_sum + kernel[shift_by] * padded[shift_by : shift_by + length]
        tap_grads.append(
            jnp.sum(conv_grad * extended[taps - 1 - shift_by : taps - 1 - shift_by + length], 0)
        )
    proj_grad = proj_sum.astype(jnp.bfloat16)
    conv_local = jnp.stack(tap_grads, 0)
    conv_w_grad, rate_total, gate_a_b_grad, gate_i_b_grad, gate_a_w_grad, gate_i_w_grad = (
        lax.psum(conv_local.astype(jnp.bfloat16), "ctx").astype(jnp.float32),
        lax.psum(rate_local.astype(jnp.bfloat16), "ctx").astype(jnp.float32),
        lax.psum(bias_a_local.astype(jnp.bfloat16), "ctx").astype(jnp.float32),
        lax.psum(bias_i_local.astype(jnp.bfloat16), "ctx").astype(jnp.float32),
        lax.psum(gate_a_local.astype(jnp.bfloat16), "ctx").astype(jnp.float32),
        lax.psum(gate_i_local.astype(jnp.bfloat16), "ctx").astype(jnp.float32),
    )
    decay_grad = rate_total * -jax.nn.sigmoid(-decay_param)
    tokens_grad = sum_at_owner(matmul_nt(proj_grad, w_in).astype(jnp.bfloat16), "mp", 0).astype(
        jnp.bfloat16
    )
    w_in_grad, w_out_grad = tuple(
        (
            part.astype(jnp.float32)
            for part in one_scatter(
                (
                    matmul_tn(token_block, proj_grad).astype(jnp.bfloat16),
                    matmul_tn(gated_out, grad_block).astype(jnp.bfloat16),
                ),
                "ctx",
                (0, 1),
            )
        )
    )
    return (
        tokens_grad,
        branch_grad,
        w_in_grad,
        w_out_grad,
        conv_w_grad,
        gate_a_w_grad,
        gate_a_b_grad,
        gate_i_w_grad,
        gate_i_b_grad,
        decay_grad,
    )


def solution(mesh):
    placed = (
        P(("ctx", "mp"), None),
        P("ctx", "mp"),
        P(("ctx", "mp"), None),
        P(None, "mp"),
        P(None, "mp"),
        P("mp", None, None),
        P("mp"),
        P("mp", None, None),
        P("mp"),
        P("mp"),
        P("mp", None),
        P("mp"),
        P(None, "mp"),
    )
    return jax.shard_map(
        shards,
        mesh=mesh,
        in_specs=placed,
        out_specs=(
            P(("ctx", "mp"), None),
            P("ctx", "mp"),
            P("ctx", "mp"),
            P("mp", "ctx"),
            P(None, "mp"),
            P("mp", None, None),
            P("mp"),
            P("mp", None, None),
            P("mp"),
            P("mp"),
        ),
        check_vma=False,
    )
```

profile of v0, /device:TPU:1, one launch (start us, length us, event | category | flops | bytes accessed | tf_op | source)
XLA Modules:
  0.0 580.5 jit_solution(13929844677286968839)
XLA Ops:
  11.4 57.7 %all-gather.2.cloned.1.call-done = bf16[256,8192]{1,0:T(8,128)(2,1)} async-done(((bf16[32,8192]{1,0:T(8,128)(2,1)}), bf16[256,8192]{1,0:T(8,128)(2,1)}) %all-gather.2.cloned.1.call-update) | async-done | bytes 4194320 | tf_op jit(solution)/shard_map/all_gather | solution.py:13
  69.0 4.1 fusion.7
  73.2 3.8 collective-permute-start
  79.3 5.7 fusion.27
  85.6 2.5 slice.854
  88.1 2.5 slice.853
  159.3 2.5 slice.888
  231.6 2.5 slice.771
  257.1 8.1 %all-to-all-start.1 = ((f32[32,2,512]{2,1,0:T(2,128)}), f32[32,2,512]{2,1,0:T(2,128)}, u32[]{:S(2)}, u32[]{:S(2)}) async-start(f32[32,2,512]{2,1,0:T(2,128)} %broadcast_in_dim.48), calls=%async_computation.1 | async-start | bytes 262144 | tf_op jit(solution)/shard_map/all_to_all | solution.py:24
  278.6 2.2 pad.206
  287.2 2.6 pad.211
  289.8 3.0 slice.710
  306.0 3.4 rev.11
  309.5 2.7 rev.12
  312.9 7.5 %all-to-all-start = ((f32[32,2,512]{2,1,0:T(2,128)}), f32[32,2,512]{2,1,0:T(2,128)S(1)}, u32[]{:S(2)}, u32[]{:S(2)}) async-start(f32[32,2,512]{2,1,0:T(2,128)} %broadcast_in_dim.44), calls=%async_computation | async-start | bytes 262144 | tf_op jit(solution)/shard_map/all_to_all | solution.py:24
  322.1 6.0 %all-to-all-done = f32[32,2,512]{2,1,0:T(2,128)S(1)} async-done(((f32[32,2,512]{2,1,0:T(2,128)}), f32[32,2,512]{2,1,0:T(2,128)S(1)}, u32[]{:S(2)}, u32[]{:S(2)}) %all-to-all-start) | async-done | bytes 131104 | tf_op jit(solution)/shard_map/all_to_all | solution.py:24
  329.2 2.7 multiply_convert_fusion
  339.4 2.0 copy.62
  343.4 2.2 multiply_reduce_fusion.4
  346.4 2.3 collective-permute-start.1
  348.7 3.3 fusion
  353.0 3.4 copy.71
  356.4 2.7 copy.101
  359.7 5.0 convolution_convert_fusion.1
  364.7 5.7 reshape_reshape.3
  370.4 7.3 %pad_maximum_fusion = bf16[32,131072]{1,0:T(8,128)(2,1)} fusion(bf16[32,65536]{1,0:T(8,128)(2,1)} %bitcast.74, bf16[32,65536]{1,0:T(8,128)(2,1)} %reshape_reshape.3), kind=kLoop, calls=%fused_computation | loop fusion | flops 16777216 | bytes 16777216 | tf_op jit(solution)/shard_map/concatenate | solution.py:81
  377.7 9.0 %reshape.109 = bf16[32768,128]{1,0:T(8,128)(2,1)} reshape(bf16[32,131072]{1,0:T(8,128)(2,1)} %pad_maximum_fusion) | data formatting | bytes 16777216 | tf_op jit(solution)/shard_map/reshape | solution.py:83
  386.7 4.8 convolution_convert_fusion.2
  391.6 4.2 all-to-all-start.2
  395.8 63.6 %all-reduce.64 = (bf16[4,512]{1,0:T(4,128)(2,1)S(1)}, bf16[512]{0:T(512)(128)(2,1)S(1)}, bf16[512]{0:T(512)(128)(2,1)S(1)}, bf16[512]{0:T(512)(128)(2,1)S(1)}) all-reduce(bf16[4,512]{1,0:T(4,128)(2,1)S(1)} %pad_maximum_fusion.33, bf16[512]{0:T(512)(128)(2,1)S(1)} %get-tuple-element.24, ...), channel_id=1, replica_groups=mesh['ctx'=32,'mp'=8] {'ctx'}, use_global_device_ids=true, to_apply=%region_6.7 | all-reduce | flops 3584 | bytes 14336 | tf_op jit(solution)/shard_map/psum | solution.py:226
  461.7 6.9 %all-reduce.68.cloned.1.call-done = (bf16[2,256,256]{2,1,0:T(8,128)(2,1)}, bf16[2,256,256]{2,1,0:T(8,128)(2,1)}) async-done(((bf16[2,256,256]{2,1,0:T(8,128)(2,1)}, bf16[2,256,256]{2,1,0:T(8,128)(2,1)}), (bf16[2,256,256]{2,1,0:T(8,128)(2,1)}, bf16[2,256,256]{2,1,0:T(8,128)(2,1)})) %all-reduce.68.cloned.1.call-update) | async-done | bytes 524304 | tf_op jit(solution)/shard_map/psum | solution.py:230
  473.3 98.2 %reduce-scatter.2.cloned.1.call-done = bf16[1024,128]{1,0:T(8,128)(2,1)} async-done(((bf16[32768,128]{1,0:T(8,128)(2,1)}), bf16[1024,128]{1,0:T(8,128)(2,1)}) %reduce-scatter.2.cloned.1.call-update) | async-done | bytes 262160 | tf_op jit(solution)/shard_map/reduce_scatter | solution.py:84
  (441 shorter events, 225.2 us)
Async XLA Ops:
  7.2 71.1 %copy-start = (bf16[2,256,256]{2,1,0:T(8,128)(2,1)S(1)}, bf16[2,256,256]{2,1,0:T(8,128)(2,1)}, u32[]{:S(2)}) copy-start(bf16[2,256,256]{2,1,0:T(8,128)(2,1)} %param.18) | copy-start | bytes 786436
  7.2 61.9 %all-gather.2.cloned.1.call-start = ((), (), s32[]{:S(2)}) async-start(), calls=%async_computation.4 | async-start | bytes 4718592 | tf_op jit(solution)/shard_map/all_gather | solution.py:13
  10.4 68.8 %copy-start.28 = (f32[512]{0:T(512)}, f32[512]{0:T(512)S(1)}, u32[]{:S(2)}) copy-start(f32[512]{0:T(512)S(1)} %fusion.63) | copy-start | bytes 6148
  11.3 66.5 %copy-start.20 = (f32[1,512]{1,0:T(1,128)}, f32[1,512]{1,0:T(1,128)S(1)}, u32[]{:S(2)}) copy-start(f32[1,512]{1,0:T(1,128)S(1)} %get-tuple-element.126) | copy-start | bytes 6148
  11.3 66.5 %copy-start.22 = (f32[1,512]{1,0:T(1,128)}, f32[1,512]{1,0:T(1,128)S(1)}, u32[]{:S(2)}) copy-start(f32[1,512]{1,0:T(1,128)S(1)} %get-tuple-element.127) | copy-start | bytes 6148
  11.3 66.5 %copy-start.24 = (f32[1,512]{1,0:T(1,128)}, f32[1,512]{1,0:T(1,128)S(1)}, u32[]{:S(2)}) copy-start(f32[1,512]{1,0:T(1,128)S(1)} %get-tuple-element.128) | copy-start | bytes 6148
  11.3 66.5 %copy-start.26 = (f32[1,512]{1,0:T(1,128)}, f32[1,512]{1,0:T(1,128)S(1)}, u32[]{:S(2)}) copy-start(f32[1,512]{1,0:T(1,128)S(1)} %get-tuple-element.129) | copy-start | bytes 6148
  11.3 66.4 %copy-start.43 = (bf16[3,512]{1,0:T(4,128)(2,1)S(1)}, bf16[3,512]{1,0:T(4,128)(2,1)}, u32[]{:S(2)}) copy-start(bf16[3,512]{1,0:T(4,128)(2,1)} %param.25) | copy-start | bytes 9220
  73.2 4.5 collective-permute-start
  176.9 69.0 %copy-start.14 = (f32[63,512]{1,0:T(8,128)S(1)}, f32[63,512]{1,0:T(8,128)}, u32[]{:S(2)}) copy-start(f32[63,512]{1,0:T(8,128)} %slice.848) | copy-start | bytes 387076
  248.6 21.2 %copy-start.16 = (f32[15,512]{1,0:T(8,128)S(1)}, f32[15,512]{1,0:T(8,128)}, u32[]{:S(2)}) copy-start(f32[15,512]{1,0:T(8,128)} %slice.732) | copy-start | bytes 92164
  248.6 21.2 %copy-start.17 = (f32[15,512]{1,0:T(8,128)S(1)}, f32[15,512]{1,0:T(8,128)}, u32[]{:S(2)}) copy-start(f32[15,512]{1,0:T(8,128)} %slice.765) | copy-start | bytes 92164
  252.0 32.7 %copy-start.4 = (f32[256,512]{1,0:T(8,128)}, f32[256,512]{1,0:T(8,128)S(1)}, u32[]{:S(2)}) copy-start(f32[256,512]{1,0:T(8,128)S(1)} %pad.258) | copy-start | bytes 1572868
  252.1 34.4 %copy-start.5 = (f32[256,512]{1,0:T(8,128)}, f32[256,512]{1,0:T(8,128)S(1)}, u32[]{:S(2)}) copy-start(f32[256,512]{1,0:T(8,128)S(1)} %pad.243) | copy-start | bytes 1572868
  257.1 55.1 %all-to-all-start.1 = ((f32[32,2,512]{2,1,0:T(2,128)}), f32[32,2,512]{2,1,0:T(2,128)}, u32[]{:S(2)}, u32[]{:S(2)}) async-start(f32[32,2,512]{2,1,0:T(2,128)} %broadcast_in_dim.48), calls=%async_computation.1 | async-start | bytes 262144 | tf_op jit(solution)/shard_map/all_to_all | solution.py:24
  298.8 22.8 %copy-start.46 = (pred[32]{0:T(512)(128)(4,1)S(1)}, pred[32]{0:T(512)(128)(4,1)}, u32[]{:S(2)}) copy-start(pred[32]{0:T(512)(128)(4,1)} %iota_compare_fusion) | copy-start | bytes 100
  298.9 29.3 %copy-start.45 = (pred[32]{0:T(512)(128)(4,1)S(1)}, pred[32]{0:T(512)(128)(4,1)}, u32[]{:S(2)}) copy-start(pred[32]{0:T(512)(128)(4,1)} %iota_compare_fusion.1) | copy-start | bytes 100
  303.0 26.1 %copy-start.44 = (f32[512]{0:T(512)S(1)}, f32[512]{0:T(512)}, u32[]{:S(2)}) copy-start(f32[512]{0:T(512)} %param.24) | copy-start | bytes 6148
  312.9 20.1 %copy-start.21 = (f32[1,512]{1,0:T(1,128)S(1)}, f32[1,512]{1,0:T(1,128)}, u32[]{:S(2)}) copy-start(f32[1,512]{1,0:T(1,128)} %copy-done.20) | copy-start | bytes 6148
  312.9 20.1 %copy-start.23 = (f32[1,512]{1,0:T(1,128)S(1)}, f32[1,512]{1,0:T(1,128)}, u32[]{:S(2)}) copy-start(f32[1,512]{1,0:T(1,128)} %copy-done.22) | copy-start | bytes 6148
  312.9 20.1 %copy-start.25 = (f32[1,512]{1,0:T(1,128)S(1)}, f32[1,512]{1,0:T(1,128)}, u32[]{:S(2)}) copy-start(f32[1,512]{1,0:T(1,128)} %copy-done.24) | copy-start | bytes 6148
  312.9 20.2 %copy-start.27 = (f32[1,512]{1,0:T(1,128)S(1)}, f32[1,512]{1,0:T(1,128)}, u32[]{:S(2)}) copy-start(f32[1,512]{1,0:T(1,128)} %copy-done.26) | copy-start | bytes 6148
  312.9 20.2 %copy-start.29 = (f32[512]{0:T(512)S(1)}, f32[512]{0:T(512)}, u32[]{:S(2)}) copy-start(f32[512]{0:T(512)} %copy-done.28) | copy-start | bytes 6148
  312.9 20.1 %copy-start.31 = (f32[512]{0:T(512)S(1)}, f32[512]{0:T(512)}, u32[]{:S(2)}) copy-start(f32[512]{0:T(512)} %param.19) | copy-start | bytes 6148
  312.9 20.1 %copy-start.33 = (f32[512]{0:T(512)S(1)}, f32[512]{0:T(512)}, u32[]{:S(2)}) copy-start(f32[512]{0:T(512)} %param.21) | copy-start | bytes 6148
  312.9 15.2 %all-to-all-start = ((f32[32,2,512]{2,1,0:T(2,128)}), f32[32,2,512]{2,1,0:T(2,128)S(1)}, u32[]{:S(2)}, u32[]{:S(2)}) async-start(f32[32,2,512]{2,1,0:T(2,128)} %broadcast_in_dim.44), calls=%async_computation | async-start | bytes 262144 | tf_op jit(solution)/shard_map/all_to_all | solution.py:24
  320.5 148.2 %all-reduce.68.cloned.1.call-start = ((), (), s32[]{:S(2)}) async-start(), calls=%async_computation.6 | async-start | bytes 1048576 | tf_op jit(solution)/shard_map/psum | solution.py:230
  346.4 13.1 %collective-permute-start.1 = (f32[3,512]{1,0:T(4,128)S(1)}, f32[3,512]{1,0:T(4,128)S(1)}, u32[]{:S(2)}, u32[]{:S(2)}) collective-permute-start(f32[3,512]{1,0:T(4,128)S(1)} %slice.1047), channel_id=1, source_target_pairs={{8,0},{16,8},{24,16},{32,24},{40,32},{48,40},{56,48},{64,56},{72,6... | collective-permute-start | bytes 18440 | tf_op jit(solution)/shard_map/ppermute | solution.py:19
  359.2 212.3 %reduce-scatter.2.cloned.1.call-start = ((), (), s32[]{:S(2)}) async-start(), calls=%async_computation.5 | async-start | bytes 8650752 | tf_op jit(solution)/shard_map/reduce_scatter | solution.py:84
  386.7 74.4 %copy-start.39 = (f32[512]{0:T(512)S(1)}, f32[512]{0:T(512)}, u32[]{:S(2)}) copy-start(f32[512]{0:T(512)} %param.22) | copy-start | bytes 6148
  391.6 182.4 %copy-start.1 = (bf16[2,256,256]{2,1,0:T(8,128)(2,1)S(1)}, bf16[2,256,256]{2,1,0:T(8,128)(2,1)}, u32[]{:S(2)}) copy-start(bf16[2,256,256]{2,1,0:T(8,128)(2,1)} %param.18) | copy-start | bytes 786436
  391.6 80.7 %all-to-all-start.2 = ((bf16[8,32,4096]{2,1,0:T(8,128)(2,1)}), bf16[8,32,4096]{2,1,0:T(8,128)(2,1)S(1)}, u32[]{:S(2)}, u32[]{:S(2)}) async-start(bf16[8,32,4096]{2,1,0:T(8,128)(2,1)} %bitcast.20), calls=%async_computation.2 | async-start | bytes 4194304 | tf_op jit(solution)/shard_map/all_to_all | solution.py:74
  (23 other events, 254.9 us)
Sparse Core Ops, SparseCore 0:
  10.4 58.6 all-gather.1
  359.3 109.2 all-reduce.67
  473.2 98.2 reduce-scatter.1
where the time goes:
time: 588 us; the launch traced here: 580 us
  local copies, waits for them, and re-layouts  185 us (31%)
  waiting for transfers between devices  169 us (29%)
  other arithmetic  93.8 us (16%)
  blocking collectives  63.6 us (11%)
  matrix products  27.4 us (5%)
  starting transfers between devices  26.3 us (4%)
  between operations  15.2 us (3%)
    reduce_scatter x1, waiting for transfers between devices, one_scatter(): lax.psum_scatter(lines, axis, tiled=True).reshape(-1)  98.2 us
    slice x58, local copies, waits for them, and re-layouts, shards(): lax.associative_scan(linear_pair, (jnp.flip(decay, 0), jnp.flip(decay * s...  66.5 us
    slice x49, local copies, waits for them, and re-layouts, shards(): lax.associative_scan(linear_pair, (decay, driven), axis=0)  65.4 us
    psum x1, blocking collectives, shards(): lax.psum(conv_local.astype(jnp.bfloat16), 'ctx').astype(jnp.float32)  63.6 us
    all_gather x1, waiting for transfers between devices, sent_together(): lax.all_gather(both, axis, axis=dim, tiled=True)  57.7 us
    mul x36, other arithmetic, linear_pair(): return (earlier[0] * later[0], later[0] * earlier[1] + later[1])  30.5 us
    all_to_all x2, starting transfers between devices, copy_for_each(): return lax.all_to_all(copies, axis, split_axis=0, concat_axis=0, tiled=True)  15.7 us
  transfers between devices with their start and end apart: 8, of which 5 were waited for; matrix products, arithmetic and copies ran while one was open for 17% of the time, Pallas kernels for 0%

commit v1 on v0

v1 whole, which is shorter than its diff:
```python
import jax
import jax.numpy as jnp
from jax import lax
from jax.experimental import pallas as pl
from jax.experimental.pallas import tpu as pltpu
from jax.sharding import PartitionSpec as P

MESH = pl.DeviceIdType.MESH
F32 = jnp.float32
BF16 = jnp.bfloat16
NMP = 8
SEG = 32
CH = 512
DM = 4096
HALF = DM // 2


def matmul_tn(left, right):
    return lax.dot_general(left, right, (((0,), (0,)), ((), ())), preferred_element_type=F32)


def matmul_nt(left, right):
    return lax.dot_general(left, right, (((1,), (1,)), ((), ())), preferred_element_type=F32)


def to_segments(value):
    return jnp.transpose(value.reshape(NMP, SEG, CH), (1, 0, 2))


def from_segments(value):
    return jnp.transpose(value, (1, 0, 2)).reshape(NMP * SEG, CH)


def remote(src, dst, send_sem, recv_sem, device):
    return pltpu.make_async_remote_copy(
        src_ref=src,
        dst_ref=dst,
        send_sem=send_sem,
        recv_sem=recv_sem,
        device_id=device,
        device_id_type=MESH,
    )


class Place:
    def __init__(self):
        self.c = lax.axis_index("ctx")
        self.m = lax.axis_index("mp")
        self.k = lax.rem(self.c, 2)
        self.x = lax.rem(lax.div(self.c, 2), 4)
        self.y = lax.div(self.c, 8)

    def chip(self, y, x, k):
        return (y * 8 + x * 2 + k, self.m)

    def other_core(self):
        return self.chip(self.y, self.x, 1 - self.k)

    def along_x(self, step):
        return self.chip(self.y, lax.rem(self.x + step, 4), self.k)

    def along_y(self, step):
        return self.chip(lax.rem(self.y + step, 4), self.x, self.k)

    def along_z(self, step):
        return (self.c, lax.rem(self.m + step, NMP))

    def along_ctx(self, step):
        return (lax.rem(self.c + step, 32), self.m)


class Gather:
    def __init__(self, place, buf, send_sem, recv_sem):
        self.p, self.buf, self.ss, self.rs = place, buf, send_sem, recv_sem

    def view(self, d, s, part):
        step = (NMP - s) if d == 0 else s
        return self.buf.at[lax.rem(self.p.m + step, NMP), :, pl.ds(part * HALF, HALF)]

    def copy(self, d, s, part, at):
        view = self.view(d, at, part)
        to = self.p.along_z(1 if d == 0 else NMP - 1)
        return remote(view, view, self.ss.at[d, s, part], self.rs.at[d, s, part], to)

    def present(self, d, s, part):
        return s < 3 or part == d

    def send(self, s):
        for part in (0, 1):
            for d in (0, 1):
                if self.present(d, s, part):
                    self.copy(d, s, part, s).start()

    def arrive(self, s):
        for part in (0, 1):
            for d in (0, 1):
                if self.present(d, s, part):
                    self.copy(d, s, part, s + 1).wait_recv()
                    if s < 3 and self.present(d, s + 1, part):
                        self.copy(d, s + 1, part, s + 1).start()

    def sent(self):
        for s in range(4):
            for part in (0, 1):
                for d in (0, 1):
                    if self.present(d, s, part):
                        self.copy(d, s, part, s).wait_send()


class Fold:
    def __init__(self, place, core, row, col, send_sem, recv_sem):
        self.p = place
        self.slots = (core, row, col)
        self.ss, self.rs = send_sem, recv_sem

    def stage(self, which, value):
        p, slots = self.p, self.slots[which]
        mine = (p.k, p.x, p.y)[which]
        slots[mine] = value
        size = 2 if which == 0 else 4
        base = (0, 1, 4)[which]
        out = []
        for o in range(1, size):
            to = p.other_core() if which == 0 else (p.along_x(o) if which == 1 else p.along_y(o))
            send = remote(
                slots.at[mine], slots.at[mine], self.ss.at[base + o - 1], self.rs.at[base + o - 1], to
            )
            send.start()
            out.append((o, to))
        for o, to in out:
            came = lax.rem(mine + size - o, size)
            remote(
                slots.at[came], slots.at[came], self.ss.at[base + o - 1], self.rs.at[base + o - 1], to
            ).wait_recv()
        return out, mine, base

    def done(self, started):
        out, mine, base, which = started
        slots = self.slots[which]
        for o, to in out:
            remote(
                slots.at[mine], slots.at[mine], self.ss.at[base + o - 1], self.rs.at[base + o - 1], to
            ).wait_send()


def minus_expm1(v):
    series = 1.0 + v * (1.0 / 8.0)
    for n in (7, 6, 5, 4, 3, 2):
        series = 1.0 + v * (1.0 / n) * series
    return jnp.where(v > -0.35, -v * series, 1.0 - jnp.exp(v))


def enter(place, partners):
    barrier = pltpu.get_barrier_semaphore()
    for device in partners:
        pl.semaphore_signal(barrier, inc=1, device_id=device, device_id_type=MESH)
    pl.semaphore_wait(barrier, len(partners))


def first_kernel(
    tokens, branch, out_grad, w_in, conv_w, gate_a, gate_a_b, gate_i, gate_i_b, decay_param, w_out,
    state_init, conv_history,
    branch_grad, tok, og, proj_out, gated, conv_b, recur_b, input_b, small,
    w_in_v, w_out_v, acc, px, cv, rg, ig, dk, rem, hs, cp, ep, br, gp, cg, kv, edge_s, edge_r, edge_c,
    core_s, row_s, col_s, core_b, row_b, col_b,
    w_sem, ts, tr, gs, gr, fs, fr, bs, brs, es, er,
):
    p = Place()
    loads = [
        pltpu.make_async_copy(w_in, w_in_v, w_sem.at[0]),
        pltpu.make_async_copy(w_out, w_out_v, w_sem.at[1]),
    ]
    for load in loads:
        load.start()
    tok[p.m] = tokens[...]
    og[p.m] = out_grad[...]
    enter(
        p,
        [p.along_z(1), p.along_z(NMP - 1), p.along_ctx(1), p.along_ctx(31), p.other_core()]
        + [p.along_x(o) for o in (1, 2, 3)]
        + [p.along_y(o) for o in (1, 2, 3)],
    )
    tokens_in = Gather(p, tok, ts, tr)
    grads_in = Gather(p, og, gs, gr)
    tokens_in.send(0)

    def wide(row):
        return jnp.broadcast_to(row.reshape(1, CH), (8, CH))

    taps = conv_w[...].astype(F32)
    for j in range(4):
        kv[j] = wide(taps[j : j + 1])
    kv[4] = wide(gate_a_b[...])
    kv[5] = wide(gate_i_b[...])
    negative = wide(-decay_param[...])
    small_exp = jnp.exp(-jnp.abs(negative))
    one_more = 1.0 + small_exp
    gap = one_more - 1.0
    log_part = jnp.where(
        gap == 0.0, small_exp, jnp.log(one_more) * (small_exp / jnp.where(gap == 0.0, 1.0, gap))
    )
    kv[6] = jnp.maximum(negative, 0.0) + log_part
    br[...] = to_segments(branch[...].astype(F32))

    for s in (0, 1, 2):
        tokens_in.arrive(s)
    grads_in.send(0)
    loads[0].wait()
    tokens_in.arrive(3)

    acc[...] = jnp.zeros_like(acc)

    def project(n, carry):
        at = pl.ds(pl.multiple_of(n * 512, 512), 512)
        acc[...] += jnp.dot(
            tok[:, :, at].reshape(256, 512), w_in_v[at, :], preferred_element_type=F32
        )
        return carry

    lax.fori_loop(0, 8, project, 0)
    edge_s[...] = acc[pl.ds(240, 16), :].astype(BF16)
    forward_edge = remote(edge_s, edge_r, es.at[0], er.at[0], p.along_ctx(1))
    forward_edge.start()
    px[pl.ds(3, 32)] = to_segments(acc[...].astype(BF16).astype(F32))
    grads_in.arrive(0)

    lane8 = lax.broadcasted_iota(jnp.int32, (8, CH), 0)
    forward_edge.wait_recv()
    first = p.c == 0
    before = edge_r[...].astype(F32)[13:16]
    before = jnp.where(first, conv_history[...].astype(F32), before)
    for j in range(3):
        turned = pltpu.roll(px[32 + j], 1, 0)
        px[j] = jnp.where(lane8 == 0, wide(before[j : j + 1]), turned)

    def convolve(n, carry):
        total = kv[0] * px[pl.ds(2 * n + 3, 2)]
        for j in (1, 2, 3):
            total = total + kv[j] * px[pl.ds(2 * n + 3 - j, 2)]
        rounded = total.astype(BF16)
        cv[pl.ds(2 * n, 2)] = rounded.astype(F32)
        conv_b[pl.ds(pl.multiple_of(16 * n, 16), 16), :] = rounded.reshape(16, CH)
        return carry

    lax.fori_loop(0, 16, convolve, 0)
    for b in (0, 1):
        cols = pl.ds(b * 256, 256)
        rg[:, :, cols] = jnp.dot(
            conv_b[:, cols], gate_a[b], preferred_element_type=F32
        ).reshape(32, 8, 256)
        ig[:, :, cols] = jnp.dot(
            conv_b[:, cols], gate_i[b], preferred_element_type=F32
        ).reshape(32, 8, 256)

    def gates(n, carry):
        h, c = carry
        at = pl.ds(2 * n, 2)
        recur = jax.nn.sigmoid(rg[at] + kv[4])
        inp = jax.nn.sigmoid(ig[at] + kv[5])
        log_decay = -8.0 * recur * kv[6]
        decay = jnp.exp(log_decay)
        remain = minus_expm1(2.0 * log_decay)
        rg[at] = recur
        ig[at] = inp
        dk[at] = decay
        rem[at] = remain
        driven = jnp.sqrt(remain) * inp * cv[at]
        for t in (0, 1):
            h = decay[t] * h + driven[t]
            c = decay[t] * c
            hs[2 * n + 1 + t] = h
            cp[2 * n + t] = c
        return h, c

    h, c = lax.fori_loop(0, 16, gates, (jnp.zeros((8, CH), F32), jnp.ones((8, CH), F32)))
    c_seg = c
    for sh in (1, 2, 4):
        ok = lane8 >= sh
        h, c = (
            jnp.where(ok, h + c * pltpu.roll(h, sh, 0), h),
            jnp.where(ok, c * pltpu.roll(c, sh, 0), c),
        )
    c_before = jnp.where(lane8 == 0, 1.0, pltpu.roll(c, 1, 0))
    h_before = jnp.where(lane8 == 0, 0.0, pltpu.roll(h, 1, 0))
    states = Fold(p, core_s, row_s, col_s, fs, fr)
    pair = jnp.where(lane8 < 4, wide(c[7:8]), wide(h[7:8]))

    def both(slot):
        value = slot
        return wide(value[0:1]), wide(value[4:5])

    held = [states.stage(0, pair) + (0,)]
    grads_in.arrive(1)

    def suffix(n, e):
        ep[31 - n] = e
        return e * dk[31 - n]

    lax.fori_loop(0, 32, suffix, jnp.ones((8, CH), F32))
    c0, h0 = both(core_s[0])
    c1, h1 = both(core_s[1])
    held.append(states.stage(1, jnp.where(lane8 < 4, c0 * c1, c1 * h0 + h1)) + (1,))
    cr, hr = jnp.ones((8, CH), F32), jnp.zeros((8, CH), F32)
    for o in range(4):
        co, ho = both(row_s[o])
        cr, hr = cr * co, co * hr + ho
    held.append(states.stage(2, jnp.where(lane8 < 4, cr, hr)) + (2,))
    state = wide(state_init[...])
    for o in range(4):
        co, ho = both(col_s[o])
        state = jnp.where(o < p.y, co * state + ho, state)
    for o in range(4):
        co, ho = both(row_s[o])
        state = jnp.where(o < p.x, co * state + ho, state)
    state = jnp.where(p.k == 1, c0 * state + h0, state)
    seg_state = h_before + c_before * state
    hs[0] = seg_state

    def finish_states(n, carry):
        at = pl.ds(2 * n, 2)
        value = hs[pl.ds(2 * n + 1, 2)] + cp[at] * seg_state
        hs[pl.ds(2 * n + 1, 2)] = value
        cp[at] = value * br[at]
        return carry

    lax.fori_loop(0, 16, finish_states, 0)
    gated[...] = from_segments(cp[...]).astype(BF16)

    grads_in.arrive(2)
    loads[1].wait()
    grads_in.arrive(3)
    acc[...] = jnp.zeros_like(acc)

    def grad_product(n, carry):
        at = pl.ds(pl.multiple_of(n * 512, 512), 512)
        acc[...] += matmul_nt(og[:, :, at].reshape(256, 512), w_out_v[:, at])
        return carry

    lax.fori_loop(0, 8, grad_product, 0)
    gp[...] = to_segments(acc[...])

    def backward(n, b):
        i = 31 - n
        g = gp[i]
        cp[i] = g * hs[i + 1]
        a = g * br[i] + b
        gp[i] = a
        return dk[i] * a

    b = lax.fori_loop(0, 32, backward, jnp.zeros((8, CH), F32))
    c = c_seg
    for sh in (1, 2, 4):
        ok = lane8 < 8 - sh
        b, c = (
            jnp.where(ok, b + c * pltpu.roll(b, 8 - sh, 0), b),
            jnp.where(ok, c * pltpu.roll(c, 8 - sh, 0), c),
        )
    c_after = jnp.where(lane8 == 7, 1.0, pltpu.roll(c, 7, 0))
    b_after = jnp.where(lane8 == 7, 0.0, pltpu.roll(b, 7, 0))
    adjoints = Fold(p, core_b, row_b, col_b, bs, brs)
    held_b = [adjoints.stage(0, wide(b[0:1])) + (0,)]
    b0, b1 = core_b[0], core_b[1]
    held_b.append(adjoints.stage(1, b0 + c0 * b1) + (1,))
    row = jnp.zeros((8, CH), F32)
    for o in (3, 2, 1, 0):
        row = row_b[o] + both(row_s[o])[0] * row
    held_b.append(adjoints.stage(2, row) + (2,))
    branch_grad[...] = from_segments(cp[...]).astype(BF16)
    later = jnp.zeros((8, CH), F32)
    for o in (3, 2, 1, 0):
        later = jnp.where(o > p.y, col_b[o] + both(col_s[o])[0] * later, later)
    for o in (3, 2, 1, 0):
        later = jnp.where(o > p.x, row_b[o] + both(row_s[o])[0] * later, later)
    later = jnp.where(p.k == 0, b1 + c1 * later, later)
    seg_later = b_after + c_after * later

    def gate_grads(n, carry):
        sum_a, sum_i, sum_r = carry
        at = pl.ds(2 * n, 2)
        adjoint = gp[at] + ep[at] * seg_later
        decay, remain, inp, recur, wide_conv = dk[at], rem[at], ig[at], rg[at], cv[at]
        scaler = jnp.sqrt(remain)
        scaler_grad = adjoint * inp * wide_conv
        log_grad = adjoint * hs[at] * decay - 2.0 * decay * decay * scaler_grad / jnp.sqrt(
            jnp.maximum(4.0 * remain, 1e-06)
        )
        recur_pre = (log_grad * (-8.0 * kv[6]) * recur * (1.0 - recur)).astype(BF16)
        input_pre = (scaler_grad * scaler * (1.0 - inp)).astype(BF16)
        flat = pl.ds(pl.multiple_of(16 * n, 16), 16)
        recur_b[flat, :] = recur_pre.reshape(16, CH)
        input_b[flat, :] = input_pre.reshape(16, CH)
        cg[at] = adjoint * scaler * inp
        return (
            sum_a + jnp.sum(recur_pre.astype(F32), 0),
            sum_i + jnp.sum(input_pre.astype(F32), 0),
            sum_r + jnp.sum(log_grad * (-8.0 * recur), 0),
        )

    zero = jnp.zeros((8, CH), F32)
    sum_a, sum_i, sum_r = lax.fori_loop(0, 16, gate_grads, (zero, zero, zero))
    for b in (0, 1):
        cols = pl.ds(b * 256, 256)
        cg[pl.ds(0, 32), :, cols] += (
            matmul_nt(recur_b[:, cols], gate_a[b]) + matmul_nt(input_b[:, cols], gate_i[b])
        ).reshape(32, 8, 256)
    backward_edge = remote(cg.at[pl.ds(0, 3)], edge_c, es.at[1], er.at[1], p.along_ctx(31))
    backward_edge.start()
    backward_edge.wait_recv()
    for j in range(3):
        turned = pltpu.roll(cg[j], 7, 0)
        came = jnp.where(p.c == 31, 0.0, wide(edge_c[j][0:1]))
        cg[32 + j] = jnp.where(lane8 == 7, came, turned)

    def proj_grads(n, carry):
        at = pl.ds(2 * n, 2)
        own = cg[at]
        total = kv[0] * own
        for j in (1, 2, 3):
            total = total + kv[j] * cg[pl.ds(2 * n + j, 2)]
        cp[at] = total
        return tuple(
            carry[j] + jnp.sum(own * px[pl.ds(2 * n + 3 - j, 2)], 0) for j in range(4)
        )

    tap_sums = lax.fori_loop(0, 16, proj_grads, (zero, zero, zero, zero))
    proj_out[...] = from_segments(cp[...]).astype(BF16)
    rows = [jnp.sum(v, 0, keepdims=True) for v in (*tap_sums, sum_r, sum_a, sum_i)]
    small[...] = jnp.concatenate(rows + [jnp.zeros((1, CH), F32)], 0)

    tokens_in.sent()
    grads_in.sent()
    for started in held:
        states.done(started)
    for started in held_b:
        adjoints.done(started)
    forward_edge.wait_send()
    backward_edge.wait_send()


def call_first(*args):
    def vm(shape, dtype):
        return pltpu.VMEM(shape, dtype)

    seg = (32, 8, CH)
    tile = (8, CH)
    dma = pltpu.SemaphoreType.DMA
    S = jax.ShapeDtypeStruct
    outs = (
        S((256, CH), BF16),
        S((8, 32, DM), BF16),
        S((8, 32, DM), BF16),
        S((256, CH), BF16),
        S((256, CH), BF16),
        S((256, CH), BF16),
        S((256, CH), BF16),
        S((256, CH), BF16),
        S((8, CH), F32),
    )
    big = {3, 10}
    return pl.pallas_call(
        first_kernel,
        out_shape=outs,
        in_specs=[
            pl.BlockSpec(memory_space=pl.ANY if n in big else pltpu.VMEM) for n in range(13)
        ],
        out_specs=tuple(pl.BlockSpec(memory_space=pltpu.VMEM) for _ in outs),
        scratch_shapes=[
            vm((DM, CH), BF16),
            vm((CH, DM), BF16),
            vm((256, CH), F32),
            vm((35, 8, CH), F32),
            *[vm(seg, F32) for _ in range(5)],
            vm((33, 8, CH), F32),
            *[vm(seg, F32) for _ in range(4)],
            vm((35, 8, CH), F32),
            vm((7, 8, CH), F32),
            vm((16, CH), BF16),
            vm((16, CH), BF16),
            vm((3, 8, CH), F32),
            vm((2, *tile), F32),
            vm((4, *tile), F32),
            vm((4, *tile), F32),
            vm((2, *tile), F32),
            vm((4, *tile), F32),
            vm((4, *tile), F32),
            dma((2,)),
            dma((2, 4, 2)),
            dma((2, 4, 2)),
            dma((2, 4, 2)),
            dma((2, 4, 2)),
            dma((7,)),
            dma((7,)),
            dma((7,)),
            dma((7,)),
            dma((2,)),
            dma((2,)),
        ],
        compiler_params=pltpu.CompilerParams(
            collective_id=0, has_side_effects=True, vmem_limit_bytes=56 << 20
        ),
    )(*args)


def cut_along(value, dim, peers):
    lengths = value.shape
    parts = value.reshape(*lengths[:dim], peers, lengths[dim] // peers, *lengths[dim + 1 :])
    return jnp.moveaxis(parts, dim, 0)


def sum_at_owner(value, axis, dim):
    peers = lax.axis_size(axis)
    parts = lax.all_to_all(cut_along(value, dim, peers), axis, 0, 0, tiled=True)
    return jnp.sum(parts.astype(jnp.float32), axis=0)


def one_scatter(arrays, axis, dims):
    peers = lax.axis_size(axis)
    parts = [cut_along(a, dim, peers) for a, dim in zip(arrays, dims)]
    lines = jnp.concatenate([b.reshape(peers, -1) for b in parts], axis=1)
    rows = max(16, -(-lines.shape[1] // 1024) * 8)
    lines = jnp.pad(lines, ((0, 0), (0, rows * 128 - lines.shape[1]))).reshape(-1, 128)
    ravelled, at, gathered = (lax.psum_scatter(lines, axis, tiled=True).reshape(-1), 0, [])
    for b in parts:
        part = b[0]
        gathered.append(ravelled[at : at + part.size].reshape(part.shape))
        at += part.size
    return tuple(gathered)


def shards(tokens, branch, out_grad, w_in, conv_w, gate_a_w, gate_a_b, gate_i_w, gate_i_b, decay_param, w_out, state_init, conv_history):
    branch_grad, tok, og, proj_grad, gated_out, conv_out, recur_pre, input_pre, small = call_first(
        tokens, branch, out_grad, w_in, conv_w, gate_a_w, gate_a_b, gate_i_w, gate_i_b, decay_param,
        w_out, state_init, conv_history,
    )
    token_block, grad_block = tok.reshape(256, DM), og.reshape(256, DM)
    conv_blocks = conv_out.reshape(256, 2, 256)
    recur_blocks = recur_pre.reshape(256, 2, 256)
    input_blocks = input_pre.reshape(256, 2, 256)
    gate_a_local = jnp.einsum("thb,thc->hbc", conv_blocks, recur_blocks, preferred_element_type=F32)
    gate_i_local = jnp.einsum("thb,thc->hbc", conv_blocks, input_blocks, preferred_element_type=F32)
    sums = lax.psum(small, "ctx")
    gate_a_w_grad = lax.psum(gate_a_local.astype(BF16), "ctx").astype(F32)
    gate_i_w_grad = lax.psum(gate_i_local.astype(BF16), "ctx").astype(F32)
    conv_w_grad, rate_total, gate_a_b_grad, gate_i_b_grad = sums[:4], sums[4], sums[5], sums[6]
    decay_grad = rate_total * -jax.nn.sigmoid(-decay_param)
    tokens_grad = sum_at_owner(matmul_nt(proj_grad, w_in).astype(jnp.bfloat16), "mp", 0).astype(
        jnp.bfloat16
    )
    w_in_grad, w_out_grad = tuple(
        (
            part.astype(jnp.float32)
            for part in one_scatter(
                (
                    matmul_tn(token_block, proj_grad).astype(jnp.bfloat16),
                    matmul_tn(gated_out, grad_block).astype(jnp.bfloat16),
                ),
                "ctx",
                (0, 1),
            )
        )
    )
    return (
        tokens_grad,
        branch_grad,
        w_in_grad,
        w_out_grad,
        conv_w_grad,
        gate_a_w_grad,
        gate_a_b_grad,
        gate_i_w_grad,
        gate_i_b_grad,
        decay_grad,
    )


def solution(mesh):
    placed = (
        P(("ctx", "mp"), None),
        P("ctx", "mp"),
        P(("ctx", "mp"), None),
        P(None, "mp"),
        P(None, "mp"),
        P("mp", None, None),
        P("mp"),
        P("mp", None, None),
        P("mp"),
        P("mp"),
        P("mp", None),
        P("mp"),
        P(None, "mp"),
    )
    return jax.shard_map(
        shards,
        mesh=mesh,
        in_specs=placed,
        out_specs=(
            P(("ctx", "mp"), None),
            P("ctx", "mp"),
            P("ctx", "mp"),
            P("mp", "ctx"),
            P(None, "mp"),
            P("mp", None, None),
            P("mp"),
            P("mp", None, None),
            P("mp"),
            P("mp"),
        ),
        check_vma=False,
    )
```

time: 588 us -> 313 us (0.53); the launches traced: 580 us -> 312 us
  local copies, waits for them, and re-layouts: 185 us -> 22.2 us
  waiting for transfers between devices: 169 us -> 42.8 us
  other arithmetic: 93.8 us -> 14.2 us
  Pallas kernels: 0 us -> 75.8 us
  blocking collectives: 63.6 us -> 124 us
  starting transfers between devices: 26.3 us -> 4.28 us
  matrix products: 27.4 us -> 14.8 us
    slice x148 -> x2, local copies, waits for them, and re-layouts: 135 us -> 1.19 us  [the longest x1 0.6 us: shards(): sums[:4]]
    pallas_call x0 -> x1, Pallas kernels: none -> 75.8 us  [call_first(): pl.pallas_call(first_kernel, out_shape=outs, in_specs=[pl.BlockSpec(memor...]
    psum x1, blocking collectives: 63.6 us -> 124 us  [shards(): sums = lax.psum(small, 'ctx')]
    all_gather x1 -> x0, waiting for transfers between devices: 57.7 us -> none  [sent_together(): lax.all_gather(both, axis, axis=dim, tiled=True)]
    reduce_scatter x1, waiting for transfers between devices: 98.2 us -> 42.7 us  [one_scatter(): lax.psum_scatter(lines, axis, tiled=True).reshape(-1)]
    mul x37 -> x0, other arithmetic: 31.2 us -> none  [the longest x36 30.5 us: linear_pair(): return (earlier[0] * later[0], later[0] * earlier[1] + later[1])]
    concatenate x29 -> x0, other arithmetic: 21.6 us -> none  [the longest x13 11 us: shards(): lax.associative_scan(linear_pair, (jnp.flip(decay, 0), jnp.flip(decay * s...]
    all_to_all x2 -> x0, starting transfers between devices: 15.7 us -> none  [copy_for_each(): return lax.all_to_all(copies, axis, split_axis=0, concat_axis=0, tiled=True)]
  transfers between devices with their start and end apart: 8 -> 3, of which waited for: 5 -> 1; matrix products, arithmetic and copies ran while one was open for 17% -> 14% of each run, Pallas kernels for 0% -> 0%
where the time goes in v1:
time: 313 us; the launch traced here: 312 us
  blocking collectives  124 us (40%)
  Pallas kernels  75.8 us (24%)
  waiting for transfers between devices  42.8 us (14%)
  local copies, waits for them, and re-layouts  22.2 us (7%)
  matrix products  14.8 us (5%)
  other arithmetic  14.2 us (5%)
  between operations  14.1 us (5%)
  starting transfers between devices  4.28 us (1%)
    psum x1, blocking collectives, shards(): sums = lax.psum(small, 'ctx')  124 us
    pallas_call x1, Pallas kernels, call_first(): pl.pallas_call(first_kernel, out_shape=outs, in_specs=[pl.BlockSpec(memor...  75.8 us
    reduce_scatter x1, waiting for transfers between devices, one_scatter(): lax.psum_scatter(lines, axis, tiled=True).reshape(-1)  42.7 us
    reshape x1, local copies, waits for them, and re-layouts, one_scatter(): jnp.pad(lines, ((0, 0), (0, rows * 128 - lines.shape[1]))).reshape(-1, 128)  8.91 us
    concatenate x1, other arithmetic, one_scatter(): lines = jnp.concatenate([b.reshape(peers, -1) for b in parts], axis=1)  7.26 us
  transfers between devices with their start and end apart: 3, of which 1 were waited for; matrix products, arithmetic and copies ran while one was open for 14% of the time, Pallas kernels for 0%

profile of v1, /device:TPU:1, one launch (start us, length us, event | category | flops | bytes accessed | tf_op | source)
XLA Modules:
  0.0 312.2 jit_solution(5012826469639128010)
XLA Ops:
  7.2 0.0 all-reduce.3.cloned.1.call-start
  7.2 75.8 %shard_map.204 = (bf16[256,512]{1,0:T(8,128)(2,1)}, bf16[8,32,4096]{2,1,0:T(8,128)(2,1)}, bf16[8,32,4096]{2,1,0:T(8,128)(2,1)}, bf16[256,512]{1,0:T(8,128)(2,1)}...) custom-call(bf16[32,4096]{1,0:T(8,128)(2,1)} %tokens.1, ...), custom_call_target="tpu_custom_call" | custom-call | tf_op jit(solution)/shard_map/pallas_call | solution.py:460
  83.0 1.1 copy.28
  84.1 1.9 convolution_convert_fusion.4
  86.0 1.9 convolution_convert_fusion.3
  87.9 0.0 all-reduce.3.cloned.1.call-update
  87.9 0.0 reduce-scatter.2.cloned.1.call-start
  87.9 3.0 fusion
  90.9 1.3 copy.32
  92.2 0.0 copy-start
  92.2 2.7 copy.42
  94.9 3.3 %convolution_convert_fusion.1 = bf16[4096,512]{1,0:T(8,128)(2,1)} fusion(bf16[256,4096]{1,0:T(8,128)(2,1)S(1)} %bitcast.34, bf16[256,512]{1,0:T(8,128)(2,1)S(1)} %copy-done.1), kind=kOutput, calls=%fused_computation.2 | convolution fusion | flops 1075838976 | bytes 6553600 | tf_op jit(solution)/shard_map/dot_general | solution.py:19
  98.1 5.7 %reshape_reshape.3 = bf16[32,65536]{1,0:T(8,128)(2,1)} reshape(bf16[4096,512]{1,0:T(8,128)(2,1)} %convolution_convert_fusion.1) | data formatting | bytes 8388608 | tf_op jit(solution)/shard_map/reshape;reshape | solution.py:519
  103.8 7.3 %pad_maximum_fusion = bf16[32,131072]{1,0:T(8,128)(2,1)} fusion(bf16[32,65536]{1,0:T(8,128)(2,1)} %bitcast.33, bf16[32,65536]{1,0:T(8,128)(2,1)} %reshape_reshape.3), kind=kLoop, calls=%fused_computation | loop fusion | flops 16777216 | bytes 16777216 | tf_op jit(solution)/shard_map/concatenate | solution.py:519
  111.1 8.9 %reshape.61 = bf16[32768,128]{1,0:T(8,128)(2,1)} reshape(bf16[32,131072]{1,0:T(8,128)(2,1)} %pad_maximum_fusion) | data formatting | bytes 16777216 | tf_op jit(solution)/shard_map/reshape | solution.py:521
  120.0 0.0 reduce-scatter.2.cloned.1.call-update
  120.0 0.0 copy-start.4
  120.0 4.8 %convolution_convert_fusion.2 = bf16[256,4096]{1,0:T(8,128)(2,1)} fusion(bf16[256,512]{1,0:T(8,128)(2,1)S(1)} %copy-done.1, bf16[4096,512]{1,0:T(8,128)(2,1)} %w_in.1), kind=kOutput, calls=%fused_computation.3 | convolution fusion | flops 1074790400 | bytes 6553600 | tf_op jit(solution)/shard_map/dot_general | solution.py:23
  124.9 4.2 %all-to-all-start = ((bf16[8,32,4096]{2,1,0:T(8,128)(2,1)}), bf16[8,32,4096]{2,1,0:T(8,128)(2,1)S(1)}, u32[]{:S(2)}, u32[]{:S(2)}) async-start(bf16[8,32,4096]{2,1,0:T(8,128)(2,1)} %bitcast), calls=%async_computation | async-start | bytes 4194304 | tf_op jit(solution)/shard_map/all_to_all | solution.py:512
  129.1 124.0 %psum.21 = f32[8,512]{1,0:T(8,128)S(1)} all-reduce(f32[8,512]{1,0:T(8,128)S(1)} %copy-done.3), channel_id=1, replica_groups=mesh['ctx'=32,'mp'=8] {'ctx'}, use_global_device_ids=true, to_apply=%region_2.0 | all-reduce | flops 4096 | bytes 32768 | tf_op jit(solution)/shard_map/psum | solution.py:541
  253.1 0.6 slice.28
  253.7 0.6 fusion.5
  254.3 0.6 negate_multiply_fusion
  254.9 1.8 convert_element_type.39
  256.6 1.8 convert_element_type.41
  258.4 0.0 all-to-all-done
  258.4 1.1 reduce_sum.12
  259.5 42.7 %reduce-scatter.2.cloned.1.call-done = bf16[1024,128]{1,0:T(8,128)(2,1)} async-done(((bf16[32768,128]{1,0:T(8,128)(2,1)}), bf16[1024,128]{1,0:T(8,128)(2,1)}) %reduce-scatter.2.cloned.1.call-update) | async-done | bytes 262160 | tf_op jit(solution)/shard_map/reduce_scatter | solution.py:522
  302.2 1.7 slice_convert_fusion
  303.9 0.7 reshape.65
  304.6 0.0 copy-done.2
  304.7 0.7 copy.46
  (8 shorter events, 0.0 us)
Async XLA Ops:
  7.2 247.7 %all-reduce.3.cloned.1.call-start = ((), (), s32[]{:S(2)}) async-start(), calls=%async_computation.3 | async-start | bytes 1048576 | tf_op jit(solution)/shard_map/psum | solution.py:542
  87.9 214.3 %reduce-scatter.2.cloned.1.call-start = ((), (), s32[]{:S(2)}) async-start(), calls=%async_computation.2 | async-start | bytes 8650752 | tf_op jit(solution)/shard_map/reduce_scatter | solution.py:522
  92.2 2.7 copy-start
  92.2 2.7 copy-start.1
  120.0 9.1 %copy-start.3 = (f32[8,512]{1,0:T(8,128)S(1)}, f32[8,512]{1,0:T(8,128)}, u32[]{:S(2)}) copy-start(f32[8,512]{1,0:T(8,128)} %get-tuple-element.24) | copy-start | bytes 49156
  120.0 134.3 %copy-start.4 = (f32[512]{0:T(512)S(1)}, f32[512]{0:T(512)}, u32[]{:S(2)}) copy-start(f32[512]{0:T(512)} %decay_param.1) | copy-start | bytes 6148
  124.9 179.8 %copy-start.2 = (bf16[256,512]{1,0:T(8,128)(2,1)S(1)}, bf16[256,512]{1,0:T(8,128)(2,1)}, u32[]{:S(2)}) copy-start(bf16[256,512]{1,0:T(8,128)(2,1)} %get-tuple-element.46) | copy-start | bytes 786436
  124.9 133.6 %all-to-all-start = ((bf16[8,32,4096]{2,1,0:T(8,128)(2,1)}), bf16[8,32,4096]{2,1,0:T(8,128)(2,1)S(1)}, u32[]{:S(2)}, u32[]{:S(2)}) async-start(bf16[8,32,4096]{2,1,0:T(8,128)(2,1)} %bitcast), calls=%async_computation | async-start | bytes 4194304 | tf_op jit(solution)/shard_map/all_to_all | solution.py:512
Sparse Core Ops, SparseCore 0:
  88.0 111.3 all-reduce.2
  203.9 98.2 reduce-scatter.1

commit v2 on v1

--- a/solution.py
+++ b/solution.py
@@ -113,34 +113,307 @@
         self.slots = (core, row, col)
         self.ss, self.rs = send_sem, recv_sem
 
-    def stage(self, which, value):
+    def copies(self, which, arriving):
         p, slots = self.p, self.slots[which]
         mine = (p.k, p.x, p.y)[which]
-        slots[mine] = value
         size = 2 if which == 0 else 4
         base = (0, 1, 4)[which]
-        out = []
+        found = []
         for o in range(1, size):
             to = p.other_core() if which == 0 else (p.along_x(o) if which == 1 else p.along_y(o))
-            send = remote(
-                slots.at[mine], slots.at[mine], self.ss.at[base + o - 1], self.rs.at[base + o - 1], to
-            )
-            send.start()
-            out.append((o, to))
-        for o, to in out:
-            came = lax.rem(mine + size - o, size)
+            slot = slots.at[lax.rem(mine + size - o, size) if arriving else mine]
+            sems = self.ss.at[base + o - 1], self.rs.at[base + o - 1]
+            found.append(remote(slot, slot, *sems, to))
+        return found
+
+    def start(self, which, value):
+        self.slots[which][(self.p.k, self.p.x, self.p.y)[which]] = value
+        for copy in self.copies(which, False):
+            copy.start()
+
+    def finish(self, which):
+        for copy in self.copies(which, True):
+            copy.wait_recv()
+
+    def drain(self):
+        for which in range(3):
+            for copy in self.copies(which, False):
+                copy.wait_send()
+
+
+class CorePair:
+    def __init__(self, place, src, dst, send_sem, recv_sem):
+        self.copy = remote(src, dst, send_sem, recv_sem, place.other_core())
+        self.start, self.finish, self.drain = (
+            self.copy.start, self.copy.wait_recv, self.copy.wait_send
+        )
+
+
+class CoreColumns:
+    def __init__(self, place, own, other, send_sem, recv_sem):
+        self.p, self.own, self.other = place, own, other
+        self.ss, self.rs = send_sem, recv_sem
+        self.whole = remote(other, other, send_sem, recv_sem, place.other_core())
+
+    def start(self):
+        def one(j, carry):
+            src = pl.ds(pl.multiple_of((2 * j + 1 - self.p.k) * 128, 128), 128)
+            dst = pl.ds(pl.multiple_of(j * 128, 128), 128)
             remote(
-                slots.at[came], slots.at[came], self.ss.at[base + o - 1], self.rs.at[base + o - 1], to
-            ).wait_recv()
-        return out, mine, base
-
-    def done(self, started):
-        out, mine, base, which = started
-        slots = self.slots[which]
-        for o, to in out:
-            remote(
-                slots.at[mine], slots.at[mine], self.ss.at[base + o - 1], self.rs.at[base + o - 1], to
-            ).wait_send()
+                self.own.at[:, :, src], self.other.at[:, :, dst], self.ss, self.rs,
+                self.p.other_core(),
+            ).start()
+            return carry
+
+        lax.fori_loop(0, 16, one, 0)
+
+    def finish(self):
+        self.whole.wait_recv()
+
+    def drain(self):
+        self.whole.wait_send()
+
+
+class WeightSum:
+    def __init__(self, place, first_x, lhs, own, other, refs):
+        self.p, self.first_x = place, first_x
+        self.lhs, self.own, self.other = lhs, own, other
+        (self.out, self.mine, self.relay, self.ring, self.q, self.relay2, self.ring2,
+         self.ss, self.rrs, self.rs, self.ss2, self.rs2) = refs
+        self.ia, self.ib = (place.x, place.y) if first_x else (place.y, place.x)
+
+    def along(self, first, step):
+        return self.p.along_x(step) if first == self.first_x else self.p.along_y(step)
+
+    def product(self, pa, pb):
+        j = pb * 4 + pa if self.first_x else pa * 4 + pb
+        here = pl.ds(pl.multiple_of((2 * j + self.p.k) * 128, 128), 128)
+        there = pl.ds(pl.multiple_of(j * 128, 128), 128)
+        return jnp.dot(
+            self.lhs[0], self.own[:, :, here].reshape(256, 128), preferred_element_type=F32
+        ) + jnp.dot(
+            self.lhs[1], self.other[:, :, there].reshape(256, 128), preferred_element_type=F32
+        )
+
+    def relay_copy(self, pb):
+        step = jnp.where(pb < 2, 1, 3)
+        return remote(
+            self.out.at[0, pb], self.relay.at[pb], self.ss.at[0, pb], self.rrs.at[pb],
+            self.along(True, step),
+        )
+
+    def ring_copy(self, d, pb):
+        return remote(
+            self.out.at[1 + d, pb], self.ring.at[d, pb], self.ss.at[1 + d, pb], self.rs.at[d, pb],
+            self.along(True, 1 + 2 * d),
+        )
+
+    def send_relay(self):
+        def one(pb, carry):
+            self.out[0, pb] = self.product(lax.rem(self.ia + 2, 4), pb).astype(BF16)
+            self.relay_copy(pb).start()
+            return carry
+
+        lax.fori_loop(0, 4, one, 0)
+
+    def send_fresh(self):
+        def one(t, carry):
+            d = lax.div(t, 2)
+            pb = lax.rem(t + 2, 4)
+            self.out[1 + d, pb] = self.product(lax.rem(self.ia + 1 + 2 * d, 4), pb).astype(BF16)
+            self.ring_copy(d, pb).start()
+            return carry
+
+        lax.fori_loop(0, 4, one, 0)
+
+    def send_joined(self):
+        def one(pb, carry):
+            d = lax.div(pb, 2)
+            value = self.product(lax.rem(self.ia + 1 + 2 * d, 4), pb)
+            self.relay_copy(pb).wait_recv()
+            self.out[1 + d, pb] = (value + self.relay[pb].astype(F32)).astype(BF16)
+            self.ring_copy(d, pb).start()
+            return carry
+
+        lax.fori_loop(0, 4, one, 0)
+
+    def keep(self):
+        def one(pb, carry):
+            self.mine[pb] = self.product(self.ia, pb)
+            return carry
+
+        lax.fori_loop(0, 4, one, 0)
+
+    def halves(self, which):
+        place = lax.rem(self.ib + 2, 4)
+        rows = pl.ds(256 * which, 256)
+        return remote(
+            self.q.at[place, rows, :], self.relay2.at[which], self.ss2.at[which],
+            self.rs2.at[which], self.along(False, 1 + 2 * which),
+        )
+
+    def ends(self, which):
+        return remote(
+            self.q.at[lax.rem(self.ib + 1 + 2 * which, 4)], self.ring2.at[which],
+            self.ss2.at[2 + which], self.rs2.at[2 + which], self.along(False, 1 + 2 * which),
+        )
+
+    def turn(self):
+        def one(t, carry):
+            pb = lax.rem(self.ib + 2 + t, 4)
+            for d in (0, 1):
+                self.ring_copy(d, pb).wait_recv()
+            total = self.mine[pb] + self.ring[0, pb].astype(F32) + self.ring[1, pb].astype(F32)
+            self.mine[pb] = total
+            self.q[pb] = total.astype(BF16)
+            return carry
+
+        one(0, 0)
+        for which in (0, 1):
+            self.halves(which).start()
+        lax.fori_loop(1, 4, one, 0)
+
+    def join(self):
+        for which in (0, 1):
+            self.halves(which).wait_recv()
+            place = lax.rem(self.ib + 1 + 2 * which, 4)
+            rows = pl.ds(256 * which, 256)
+            self.q[place, rows, :] = (
+                self.mine[place, rows, :] + self.relay2[which].astype(F32)
+            ).astype(BF16)
+            self.ends(which).start()
+
+    def finish(self, result):
+        for which in (0, 1):
+            self.ends(which).wait_recv()
+        result[...] = self.mine[self.ib] + self.ring2[0].astype(F32) + self.ring2[1].astype(F32)
+
+    def drain(self):
+        def one(pb, carry):
+            self.relay_copy(pb).wait_send()
+            for d in (0, 1):
+                self.ring_copy(d, pb).wait_send()
+            return carry
+
+        lax.fori_loop(0, 4, one, 0)
+        for which in (0, 1):
+            self.halves(which).wait_send()
+            self.ends(which).wait_send()
+
+
+class RowSum:
+    def __init__(self, place, parts, came, send_sem, recv_sem):
+        self.p, self.parts, self.came = place, parts, came
+        self.ss, self.rs = send_sem, recv_sem
+
+    def block(self, d, s):
+        return lax.rem(self.p.m + (4 - s if d == 0 else 4 + s), NMP)
+
+    def copy(self, d, s, part):
+        cols = pl.ds(part * HALF, HALF)
+        return remote(
+            self.parts.at[self.block(d, s), :, cols], self.came.at[d, s, :, cols],
+            self.ss.at[d, s, part], self.rs.at[d, s, part], self.p.along_z(1 if d == 0 else NMP - 1),
+        )
+
+    def begin(self, part):
+        self.copy(part, 0, part).start()
+        self.copy(1 - part, 1, part).start()
+
+    def step(self, s):
+        for fresh in (True, False):
+            for d in (0, 1):
+                part = 1 - d if fresh else d
+                if fresh and s == 1:
+                    continue
+                self.copy(d, s - 1, part).wait_recv()
+                cols = pl.ds(part * HALF, HALF)
+                to = self.block(d, s)
+                self.parts[to, :, cols] = (
+                    self.parts[to, :, cols].astype(F32) + self.came[d, s - 1, :, cols].astype(F32)
+                ).astype(BF16)
+                self.copy(d, s, part).start()
+
+    def finish(self, result):
+        for d in (0, 1):
+            for part in (0, 1):
+                self.copy(d, 3, part).wait_recv()
+        result[...] = (
+            self.parts[self.p.m].astype(F32)
+            + self.came[0, 3].astype(F32)
+            + self.came[1, 3].astype(F32)
+        ).astype(BF16)
+
+    def drain(self):
+        for d in (0, 1):
+            for s in range(4):
+                for part in (0, 1):
+                    if s > 0 or part == d:
+                        self.copy(d, s, part).wait_send()
+
+
+class GateSum:
+    def __init__(self, place, parts, row, mid, col, total, send_sem, recv_sem):
+        self.p = place
+        self.parts, self.row, self.mid, self.col, self.total = parts, row, mid, col, total
+        self.ss, self.rs = send_sem, recv_sem
+
+    def copies(self, which, arriving):
+        p = self.p
+        if which == 4:
+            view = self.total.at[1 - p.k if arriving else p.k]
+            return [remote(view, view, self.ss.at[4, 0], self.rs.at[4, 0], p.other_core())]
+        found = []
+        for o in (1, 2, 3):
+            x, y = lax.rem(p.x + o, 4), lax.rem(p.y + o, 4)
+            back_x, back_y = lax.rem(p.x + 4 - o, 4), lax.rem(p.y + 4 - o, 4)
+            sems = self.ss.at[which, o - 1], self.rs.at[which, o - 1]
+            if which == 0:
+                src = self.parts.at[:, pl.ds(pl.multiple_of(x * 64, 64), 64), :]
+                dst = self.row.at[back_x if arriving else p.x]
+                found.append(remote(src, dst, *sems, p.along_x(o)))
+            elif which == 1:
+                src = self.mid.at[:, pl.ds(pl.multiple_of(y * 16, 16), 16), :]
+                dst = self.col.at[back_y if arriving else p.y]
+                found.append(remote(src, dst, *sems, p.along_y(o)))
+            elif which == 2:
+                at = p.x * 64 + (back_y if arriving else p.y) * 16
+                view = self.total.at[p.k, :, pl.ds(pl.multiple_of(at, 16), 16), :]
+                found.append(remote(view, view, *sems, p.along_y(o)))
+            else:
+                at = (back_x if arriving else p.x) * 64
+                view = self.total.at[p.k, :, pl.ds(pl.multiple_of(at, 64), 64), :]
+                found.append(remote(view, view, *sems, p.along_x(o)))
+        return found
+
+    def start(self, which):
+        p = self.p
+        if which == 0:
+            mine = pl.ds(pl.multiple_of(p.x * 64, 64), 64)
+            self.row[p.x] = self.parts[:, mine, :]
+        if which == 1:
+            total = self.row[0].astype(F32)
+            for o in (1, 2, 3):
+                total = total + self.row[o].astype(F32)
+            self.mid[...] = total.astype(BF16)
+            self.col[p.y] = self.mid[:, pl.ds(pl.multiple_of(p.y * 16, 16), 16), :]
+        if which == 2:
+            total = self.col[0].astype(F32)
+            for o in (1, 2, 3):
+                total = total + self.col[o].astype(F32)
+            at = pl.ds(pl.multiple_of(p.x * 64 + p.y * 16, 16), 16)
+            self.total[p.k, :, at, :] = total.astype(BF16)
+        for copy in self.copies(which, False):
+            copy.start()
+
+    def finish(self, which):
+        for copy in self.copies(which, True):
+            copy.wait_recv()
+
+    def drain(self):
+        for which in range(5):
+            for copy in self.copies(which, False):
+                copy.wait_send()
 
 
 def minus_expm1(v):
@@ -160,10 +433,14 @@
 def first_kernel(
     tokens, branch, out_grad, w_in, conv_w, gate_a, gate_a_b, gate_i, gate_i_b, decay_param, w_out,
     state_init, conv_history,
-    branch_grad, tok, og, proj_out, gated, conv_b, recur_b, input_b, small,
+    tokens_grad, branch_grad, w_in_t, w_out_grad, small, gate_total,
+    tok, og, proj, gated, conv_b, ri, tok_o, og_o, conv_o, ri_o, gate_p, gate_row, gate_mid, gate_col,
+    lhs_g, lhs_p, parts, came,
     w_in_v, w_out_v, acc, px, cv, rg, ig, dk, rem, hs, cp, ep, br, gp, cg, kv, edge_s, edge_r, edge_c,
     core_s, row_s, col_s, core_b, row_b, col_b,
-    w_sem, ts, tr, gs, gr, fs, fr, bs, brs, es, er,
+    core_m, row_m, col_m,
+    w_sem, ts, tr, gs, gr, fs, fr, bs, brs, es, er, ms, mr, zs, zr, ps, pr, qs, qr,
+    *sums,
 ):
     p = Place()
     loads = [
@@ -207,6 +484,19 @@
     grads_in.send(0)
     loads[0].wait()
     tokens_in.arrive(3)
+    other_tokens = CoreColumns(p, tok, tok_o, ps.at[0], pr.at[0])
+    other_grads = CoreColumns(p, og, og_o, ps.at[1], pr.at[1])
+    other_conv = CorePair(p, conv_b, conv_o, ps.at[2], pr.at[2])
+    other_gated = CorePair(p, lhs_g.at[0], lhs_g.at[1], ps.at[3], pr.at[3])
+    other_proj = CorePair(p, lhs_p.at[0], lhs_p.at[1], ps.at[4], pr.at[4])
+    other_gate = CorePair(p, ri.at[1 - p.k], ri_o, ps.at[5], pr.at[5])
+    pairs = [other_tokens, other_grads, other_conv, other_gated, other_proj, other_gate]
+    w_out_sum = WeightSum(p, False, lhs_g, og, og_o, sums[:12])
+    w_in_sum = WeightSum(p, True, lhs_p, tok, tok_o, sums[12:])
+    row_sum = RowSum(p, parts, came, zs, zr)
+    gate_sum = GateSum(p, gate_p, gate_row, gate_mid, gate_col, gate_total, qs, qr)
+    total_sum = Fold(p, core_m, row_m, col_m, ms, mr)
+    other_tokens.start()
 
     acc[...] = jnp.zeros_like(acc)
 
@@ -243,6 +533,7 @@
         return carry
 
     lax.fori_loop(0, 16, convolve, 0)
+    other_conv.start()
     for b in (0, 1):
         cols = pl.ds(b * 256, 256)
         rg[:, :, cols] = jnp.dot(
@@ -289,7 +580,7 @@
         value = slot
         return wide(value[0:1]), wide(value[4:5])
 
-    held = [states.stage(0, pair) + (0,)]
+    states.start(0, pair)
     grads_in.arrive(1)
 
     def suffix(n, e):
@@ -297,14 +588,17 @@
         return e * dk[31 - n]
 
     lax.fori_loop(0, 32, suffix, jnp.ones((8, CH), F32))
+    states.finish(0)
     c0, h0 = both(core_s[0])
     c1, h1 = both(core_s[1])
-    held.append(states.stage(1, jnp.where(lane8 < 4, c0 * c1, c1 * h0 + h1)) + (1,))
+    states.start(1, jnp.where(lane8 < 4, c0 * c1, c1 * h0 + h1))
+    states.finish(1)
     cr, hr = jnp.ones((8, CH), F32), jnp.zeros((8, CH), F32)
     for o in range(4):
         co, ho = both(row_s[o])
         cr, hr = cr * co, co * hr + ho
-    held.append(states.stage(2, jnp.where(lane8 < 4, cr, hr)) + (2,))
+    states.start(2, jnp.where(lane8 < 4, cr, hr))
+    states.finish(2)
     state = wide(state_init[...])
     for o in range(4):
         co, ho = both(col_s[o])
@@ -325,10 +619,13 @@
 
     lax.fori_loop(0, 16, finish_states, 0)
     gated[...] = from_segments(cp[...]).astype(BF16)
+    lhs_g[0] = gated[...].T
+    other_gated.start()
 
     grads_in.arrive(2)
     loads[1].wait()
     grads_in.arrive(3)
+    other_grads.start()
     acc[...] = jnp.zeros_like(acc)
 
     def grad_product(n, carry):
@@ -358,14 +655,21 @@
     c_after = jnp.where(lane8 == 7, 1.0, pltpu.roll(c, 7, 0))
     b_after = jnp.where(lane8 == 7, 0.0, pltpu.roll(b, 7, 0))
     adjoints = Fold(p, core_b, row_b, col_b, bs, brs)
-    held_b = [adjoints.stage(0, wide(b[0:1])) + (0,)]
+    adjoints.start(0, wide(b[0:1]))
+    other_gated.finish()
+    other_grads.finish()
+    w_out_sum.send_relay()
+    adjoints.finish(0)
     b0, b1 = core_b[0], core_b[1]
-    held_b.append(adjoints.stage(1, b0 + c0 * b1) + (1,))
+    adjoints.start(1, b0 + c0 * b1)
+    w_out_sum.send_fresh()
+    adjoints.finish(1)
     row = jnp.zeros((8, CH), F32)
     for o in (3, 2, 1, 0):
         row = row_b[o] + both(row_s[o])[0] * row
-    held_b.append(adjoints.stage(2, row) + (2,))
+    adjoints.start(2, row)
     branch_grad[...] = from_segments(cp[...]).astype(BF16)
+    adjoints.finish(2)
     later = jnp.zeros((8, CH), F32)
     for o in (3, 2, 1, 0):
         later = jnp.where(o > p.y, col_b[o] + both(col_s[o])[0] * later, later)
@@ -387,8 +691,8 @@
         recur_pre = (log_grad * (-8.0 * kv[6]) * recur * (1.0 - recur)).astype(BF16)
         input_pre = (scaler_grad * scaler * (1.0 - inp)).astype(BF16)
         flat = pl.ds(pl.multiple_of(16 * n, 16), 16)
-        recur_b[flat, :] = recur_pre.reshape(16, CH)
-        input_b[flat, :] = input_pre.reshape(16, CH)
+        ri[0, flat, :] = recur_pre.reshape(16, CH)
+        ri[1, flat, :] = input_pre.reshape(16, CH)
         cg[at] = adjoint * scaler * inp
         return (
             sum_a + jnp.sum(recur_pre.astype(F32), 0),
@@ -398,13 +702,15 @@
 
     zero = jnp.zeros((8, CH), F32)
     sum_a, sum_i, sum_r = lax.fori_loop(0, 16, gate_grads, (zero, zero, zero))
+    other_gate.start()
     for b in (0, 1):
         cols = pl.ds(b * 256, 256)
         cg[pl.ds(0, 32), :, cols] += (
-            matmul_nt(recur_b[:, cols], gate_a[b]) + matmul_nt(input_b[:, cols], gate_i[b])
+            matmul_nt(ri[0, :, cols], gate_a[b]) + matmul_nt(ri[1, :, cols], gate_i[b])
         ).reshape(32, 8, 256)
     backward_edge = remote(cg.at[pl.ds(0, 3)], edge_c, es.at[1], er.at[1], p.along_ctx(31))
     backward_edge.start()
+    w_out_sum.send_joined()
     backward_edge.wait_recv()
     for j in range(3):
         turned = pltpu.roll(cg[j], 7, 0)
@@ -423,16 +729,64 @@
         )
 
     tap_sums = lax.fori_loop(0, 16, proj_grads, (zero, zero, zero, zero))
-    proj_out[...] = from_segments(cp[...]).astype(BF16)
+    proj[...] = from_segments(cp[...]).astype(BF16)
+    lhs_p[0] = proj[...].T
+    other_proj.start()
+    for part in (0, 1):
+
+        def spread(n, carry):
+            at = pl.ds(pl.multiple_of(n * 512, 512), 512)
+            parts[:, :, at] = matmul_nt(proj[...], w_in_v[at, :]).astype(BF16).reshape(8, 32, 512)
+            return carry
+
+        lax.fori_loop(part * 4, part * 4 + 4, spread, 0)
+        row_sum.begin(part)
     rows = [jnp.sum(v, 0, keepdims=True) for v in (*tap_sums, sum_r, sum_a, sum_i)]
-    small[...] = jnp.concatenate(rows + [jnp.zeros((1, CH), F32)], 0)
-
+    total_sum.start(0, jnp.concatenate(rows + [jnp.zeros((1, CH), F32)], 0))
+    other_tokens.finish()
+    other_proj.finish()
+    w_in_sum.send_relay()
+    w_in_sum.send_fresh()
+    row_sum.step(1)
+    other_conv.finish()
+    other_gate.finish()
+    for b in (0, 1):
+        cols = pl.ds(b * 256, 256)
+        gate_p[b] = (
+            matmul_tn(conv_b[:, cols], ri[p.k, :, cols]) + matmul_tn(conv_o[:, cols], ri_o[:, cols])
+        ).astype(BF16)
+    gate_sum.start(0)
+    w_out_sum.keep()
+    w_out_sum.turn()
+    w_in_sum.send_joined()
+    row_sum.step(2)
+    total_sum.finish(0)
+    total_sum.start(1, core_m[0] + core_m[1])
+    gate_sum.finish(0)
+    gate_sum.start(1)
+    w_out_sum.join()
+    w_in_sum.keep()
+    row_sum.step(3)
+    total_sum.finish(1)
+    total_sum.start(2, row_m[0] + row_m[1] + row_m[2] + row_m[3])
+    w_in_sum.turn()
+    gate_sum.finish(1)
+    gate_sum.start(2)
+    w_out_sum.finish(w_out_grad)
+    gate_sum.finish(2)
+    gate_sum.start(3)
+    w_in_sum.join()
+    total_sum.finish(2)
+    small[...] = col_m[0] + col_m[1] + col_m[2] + col_m[3]
+    gate_sum.finish(3)
+    gate_sum.start(4)
+    row_sum.finish(tokens_grad)
+    w_in_sum.finish(w_in_t)
+    gate_sum.finish(4)
+    for used in (states, adjoints, total_sum, w_out_sum, w_in_sum, row_sum, gate_sum, *pairs):
+        used.drain()
     tokens_in.sent()
     grads_in.sent()
-    for started in held:
-        states.done(started)
-    for started in held_b:
-        adjoints.done(started)
     forward_edge.wait_send()
     backward_edge.wait_send()
 
@@ -446,16 +800,27 @@
     dma = pltpu.SemaphoreType.DMA
     S = jax.ShapeDtypeStruct
     outs = (
+        S((32, DM), BF16),
         S((256, CH), BF16),
-        S((8, 32, DM), BF16),
-        S((8, 32, DM), BF16),
-        S((256, CH), BF16),
-        S((256, CH), BF16),
-        S((256, CH), BF16),
-        S((256, CH), BF16),
-        S((256, CH), BF16),
+        S((CH, 128), F32),
+        S((CH, 128), F32),
         S((8, CH), F32),
+        S((2, 2, 256, 256), BF16),
     )
+    weight = [
+        vm((3, 4, CH, 128), BF16),
+        vm((4, CH, 128), F32),
+        vm((4, CH, 128), BF16),
+        vm((2, 4, CH, 128), BF16),
+        vm((4, CH, 128), BF16),
+        vm((2, 256, 128), BF16),
+        vm((2, CH, 128), BF16),
+        dma((3, 4)),
+        dma((4,)),
+        dma((2, 4)),
+        dma((4,)),
+        dma((4,)),
+    ]
     big = {3, 10}
     return pl.pallas_call(
         first_kernel,
@@ -465,6 +830,24 @@
         ],
         out_specs=tuple(pl.BlockSpec(memory_space=pltpu.VMEM) for _ in outs),
         scratch_shapes=[
+            vm((8, 32, DM), BF16),
+            vm((8, 32, DM), BF16),
+            vm((256, CH), BF16),
+            vm((256, CH), BF16),
+            vm((256, CH), BF16),
+            vm((2, 256, CH), BF16),
+            vm((8, 32, HALF), BF16),
+            vm((8, 32, HALF), BF16),
+            vm((256, CH), BF16),
+            vm((256, CH), BF16),
+            vm((2, 256, 256), BF16),
+            vm((4, 2, 64, 256), BF16),
+            vm((2, 64, 256), BF16),
+            vm((4, 2, 16, 256), BF16),
+            vm((2, CH, 256), BF16),
+            vm((2, CH, 256), BF16),
+            vm((8, 32, DM), BF16),
+            vm((2, 4, 32, DM), BF16),
             vm((DM, CH), BF16),
             vm((CH, DM), BF16),
             vm((256, CH), F32),
@@ -483,6 +866,9 @@
             vm((2, *tile), F32),
             vm((4, *tile), F32),
             vm((4, *tile), F32),
+            vm((2, *tile), F32),
+            vm((4, *tile), F32),
+            vm((4, *tile), F32),
             dma((2,)),
             dma((2, 4, 2)),
             dma((2, 4, 2)),
@@ -494,6 +880,16 @@
             dma((7,)),
             dma((2,)),
             dma((2,)),
+            dma((7,)),
+            dma((7,)),
+            dma((2, 4, 2)),
+            dma((2, 4, 2)),
+            dma((6,)),
+            dma((6,)),
+            dma((5, 3)),
+            dma((5, 3)),
+            *weight,
+            *weight,
         ],
         compiler_params=pltpu.CompilerParams(
             collective_id=0, has_side_effects=True, vmem_limit_bytes=56 << 20
@@ -501,76 +897,44 @@
     )(*args)
 
 
-def cut_along(value, dim, peers):
-    lengths = value.shape
-    parts = value.reshape(*lengths[:dim], peers, lengths[dim] // peers, *lengths[dim + 1 :])
-    return jnp.moveaxis(parts, dim, 0)
-
-
-def sum_at_owner(value, axis, dim):
-    peers = lax.axis_size(axis)
-    parts = lax.all_to_all(cut_along(value, dim, peers), axis, 0, 0, tiled=True)
-    return jnp.sum(parts.astype(jnp.float32), axis=0)
-
-
-def one_scatter(arrays, axis, dims):
-    peers = lax.axis_size(axis)
-    parts = [cut_along(a, dim, peers) for a, dim in zip(arrays, dims)]
-    lines = jnp.concatenate([b.reshape(peers, -1) for b in parts], axis=1)
-    rows = max(16, -(-lines.shape[1] // 1024) * 8)
-    lines = jnp.pad(lines, ((0, 0), (0, rows * 128 - lines.shape[1]))).reshape(-1, 128)
-    ravelled, at, gathered = (lax.psum_scatter(lines, axis, tiled=True).reshape(-1), 0, [])
-    for b in parts:
-        part = b[0]
-        gathered.append(ravelled[at : at + part.size].reshape(part.shape))
-        at += part.size
-    return tuple(gathered)
-
-
-def shards(tokens, branch, out_grad, w_in, conv_w, gate_a_w, gate_a_b, gate_i_w, gate_i_b, decay_param, w_out, state_init, conv_history):
-    branch_grad, tok, og, proj_grad, gated_out, conv_out, recur_pre, input_pre, small = call_first(
-        tokens, branch, out_grad, w_in, conv_w, gate_a_w, gate_a_b, gate_i_w, gate_i_b, decay_param,
-        w_out, state_init, conv_history,
+def last_kernel(
+    tokens_grad, branch_grad, w_in_t, w_out_grad, small, gates, decay_param,
+    o_tokens, o_branch, o_w_in, o_w_out, o_conv, o_ga, o_gab, o_gi, o_gib, o_decay,
+):
+    o_tokens[...] = tokens_grad[...]
+    o_branch[...] = branch_grad[...]
+    o_w_in[...] = w_in_t[...].T
+    o_w_out[...] = w_out_grad[...]
+    o_conv[...] = small[pl.ds(0, 4), :]
+    rows = small[...]
+    o_gab[...] = rows[5]
+    o_gib[...] = rows[6]
+    o_decay[...] = rows[4] * -jax.nn.sigmoid(-decay_param[...])
+    o_ga[...] = gates[0].astype(F32)
+    o_gi[...] = gates[1].astype(F32)
+
+
+def shards(*args):
+    results = call_first(*args)
+    S = jax.ShapeDtypeStruct
+    outs = (
+        S((32, DM), BF16),
+        S((256, CH), BF16),
+        S((128, CH), F32),
+        S((CH, 128), F32),
+        S((4, CH), F32),
+        S((2, 256, 256), F32),
+        S((CH,), F32),
+        S((2, 256, 256), F32),
+        S((CH,), F32),
+        S((CH,), F32),
     )
-    token_block, grad_block = tok.reshape(256, DM), og.reshape(256, DM)
-    conv_blocks = conv_out.reshape(256, 2, 256)
-    recur_blocks = recur_pre.reshape(256, 2, 256)
-    input_blocks = input_pre.reshape(256, 2, 256)
-    gate_a_local = jnp.einsum("thb,thc->hbc", conv_blocks, recur_blocks, preferred_element_type=F32)
-    gate_i_local = jnp.einsum("thb,thc->hbc", conv_blocks, input_blocks, preferred_element_type=F32)
-    sums = lax.psum(small, "ctx")
-    gate_a_w_grad = lax.psum(gate_a_local.astype(BF16), "ctx").astype(F32)
-    gate_i_w_grad = lax.psum(gate_i_local.astype(BF16), "ctx").astype(F32)
-    conv_w_grad, rate_total, gate_a_b_grad, gate_i_b_grad = sums[:4], sums[4], sums[5], sums[6]
-    decay_grad = rate_total * -jax.nn.sigmoid(-decay_param)
-    tokens_grad = sum_at_owner(matmul_nt(proj_grad, w_in).astype(jnp.bfloat16), "mp", 0).astype(
-        jnp.bfloat16
-    )
-    w_in_grad, w_out_grad = tuple(
-        (
-            part.astype(jnp.float32)
-            for part in one_scatter(
-                (
-                    matmul_tn(token_block, proj_grad).astype(jnp.bfloat16),
-                    matmul_tn(gated_out, grad_block).astype(jnp.bfloat16),
-                ),
-                "ctx",
-                (0, 1),
-            )
-        )
-    )
-    return (
-        tokens_grad,
-        branch_grad,
-        w_in_grad,
-        w_out_grad,
-        conv_w_grad,
-        gate_a_w_grad,
-        gate_a_b_grad,
-        gate_i_w_grad,
-        gate_i_b_grad,
-        decay_grad,
-    )
+    return pl.pallas_call(
+        last_kernel,
+        out_shape=outs,
+        in_specs=[pl.BlockSpec(memory_space=pltpu.VMEM)] * 7,
+        out_specs=tuple(pl.BlockSpec(memory_space=pltpu.VMEM) for _ in outs),
+    )(*results, args[9])
 
 
 def solution(mesh):

time: 313 us -> 129 us (0.41)
  blocking collectives: 124 us -> 0 us
  Pallas kernels: 75.8 us -> 128 us
  waiting for transfers between devices: 42.8 us -> 0 us
  local copies, waits for them, and re-layouts: 22.2 us -> 0 us
  matrix products: 14.8 us -> 0 us
  other arithmetic: 14.2 us -> 0 us
  between operations: 14.1 us -> 0.66 us
  starting transfers between devices: 4.28 us -> 0 us
    psum x1 -> x0, blocking collectives: 124 us -> none  [shards(): sums = lax.psum(small, 'ctx')]
    pallas_call x1, Pallas kernels: 75.8 us -> 126 us  [call_first(): pl.pallas_call(first_kernel, out_shape=outs, in_specs=[pl.BlockSpec(memor...]
    reduce_scatter x1 -> x0, waiting for transfers between devices: 42.7 us -> none  [one_scatter(): lax.psum_scatter(lines, axis, tiled=True).reshape(-1)]
    dot_general x5 -> x0, matrix products: 14.8 us -> none  [the longest x2 6.23 us: matmul_tn(): lax.dot_general(left, right, (((0,), (0,)), ((), ())), preferred_element_...]
    reshape x3 -> x0, local copies, waits for them, and re-layouts: 12.7 us -> none  [the longest x1 8.91 us: one_scatter(): jnp.pad(lines, ((0, 0), (0, rows * 128 - lines.shape[1]))).reshape(-1, 128)]
    concatenate x1 -> x0, other arithmetic: 7.26 us -> none  [one_scatter(): lines = jnp.concatenate([b.reshape(peers, -1) for b in parts], axis=1)]
    another operation x1 -> x0, local copies, waits for them, and re-layouts: 5.67 us -> none  [one_scatter(): lines = jnp.concatenate([b.reshape(peers, -1) for b in parts], axis=1)]
    convert_element_type x3 -> x0, other arithmetic: 5.26 us -> none  [the longest x1 1.78 us: shards(): gate_a_w_grad = lax.psum(gate_a_local.astype(BF16), 'ctx').astype(F32)]
  transfers between devices with their start and end apart: 3 -> 0, of which waited for: 1 -> 0; matrix products, arithmetic and copies ran while one was open for 14% -> 0% of each run, Pallas kernels for 0% -> 0%
where the time goes in v2:
time: 129 us
  Pallas kernels  128 us (99%)
    pallas_call x1, Pallas kernels, call_first(): pl.pallas_call(first_kernel, out_shape=outs, in_specs=[pl.BlockSpec(memor...  126 us
    pallas_call x1, Pallas kernels, shards(): pl.pallas_call(last_kernel, out_shape=outs, in_specs=[pl.BlockSpec(memory...  2.77 us

profile of v2, /device:TPU:1, one launch (start us, length us, event | category | flops | bytes accessed | tf_op | source)
XLA Modules:
  0.0 129.1 jit_solution(7102083913512916873)
XLA Ops:
  0.6 125.7 %shard_map.204 = (bf16[32,4096]{1,0:T(8,128)(2,1)}, bf16[256,512]{1,0:T(8,128)(2,1)}, f32[512,128]{1,0:T(8,128)}, f32[512,128]{1,0:T(8,128)}, f32[8,512]{1,0:T(8,128)}, /*index=5*/bf16[2,2,256,256]{3,2,1,0:T(8,128)(2,1)}) custom-call(bf16[32,4096]{1,0:T(8,128)(2,1)} %tokens.1, bf16[256,512]{1,0:T(8,128)(2,1)} %branch.1, bf16[32,4096]{1,0:T(8,128)(2,1)} %out_grad.1, ...), custom_call_target="tpu_custom_call" | custom-call | tf_op jit(solution)/shard_map/pallas_call | solution.py:825
  126.3 2.8 %shard_map.205 = (bf16[32,4096]{1,0:T(8,128)(2,1)}, bf16[256,512]{1,0:T(8,128)(2,1)}, f32[128,512]{1,0:T(8,128)}, f32[512,128]{1,0:T(8,128)}, f32[4,512]{1,0:T(4...) custom-call(bf16[32,4096]{1,0:T(8,128)(2,1)} %get-tuple-element.16.tokens_, ...), custom_call_target="tpu_custom_call" | custom-call | tf_op jit(solution)/shard_map/pallas_call | solution.py:932

commit v3 on v2

--- a/solution.py
+++ b/solution.py
@@ -141,6 +141,38 @@
                 copy.wait_send()
 
 
+class Everyone:
+    def __init__(self, place, slots, send_sem, recv_sem):
+        self.p, self.slots, self.ss, self.rs = place, slots, send_sem, recv_sem
+
+    def copy(self, o, owner):
+        slot = self.slots.at[owner]
+        return remote(slot, slot, self.ss.at[o], self.rs.at[o], self.p.along_ctx(o))
+
+    def start(self, value):
+        self.slots[self.p.c] = value
+
+        def one(o, carry):
+            self.copy(o, self.p.c).start()
+            return carry
+
+        lax.fori_loop(1, 32, one, 0)
+
+    def finish(self):
+        def one(o, carry):
+            self.copy(o, lax.rem(self.p.c + 32 - o, 32)).wait_recv()
+            return carry
+
+        lax.fori_loop(1, 32, one, 0)
+
+    def drain(self):
+        def one(o, carry):
+            self.copy(o, self.p.c).wait_send()
+            return carry
+
+        lax.fori_loop(1, 32, one, 0)
+
+
 class CorePair:
     def __init__(self, place, src, dst, send_sem, recv_sem):
         self.copy = remote(src, dst, send_sem, recv_sem, place.other_core())
@@ -179,126 +211,145 @@
         self.p, self.first_x = place, first_x
         self.lhs, self.own, self.other = lhs, own, other
         (self.out, self.mine, self.relay, self.ring, self.q, self.relay2, self.ring2,
-         self.ss, self.rrs, self.rs, self.ss2, self.rs2) = refs
+         self.ss, self.rs, self.ss2, self.rs2) = refs
         self.ia, self.ib = (place.x, place.y) if first_x else (place.y, place.x)
+        self.rows = pl.ds(0 if first_x else 256, 256)
 
     def along(self, first, step):
         return self.p.along_x(step) if first == self.first_x else self.p.along_y(step)
 
-    def product(self, pa, pb):
+    def product(self, distance, o):
+        pa, pb = lax.rem(self.ia + distance, 4), lax.rem(self.ib + o, 4)
         j = pb * 4 + pa if self.first_x else pa * 4 + pb
         here = pl.ds(pl.multiple_of((2 * j + self.p.k) * 128, 128), 128)
         there = pl.ds(pl.multiple_of(j * 128, 128), 128)
         return jnp.dot(
-            self.lhs[0], self.own[:, :, here].reshape(256, 128), preferred_element_type=F32
+            self.lhs[0, self.rows, :], self.own[:, :, here].reshape(256, 128),
+            preferred_element_type=F32,
         ) + jnp.dot(
-            self.lhs[1], self.other[:, :, there].reshape(256, 128), preferred_element_type=F32
-        )
-
-    def relay_copy(self, pb):
-        step = jnp.where(pb < 2, 1, 3)
+            self.lhs[1, self.rows, :], self.other[:, :, there].reshape(256, 128),
+            preferred_element_type=F32,
+        )
+
+    def copy(self, kind, o):
+        side = lax.rem(o, 2) if kind != 1 else 1 - lax.rem(o, 2)
+        target = self.relay.at[o] if kind == 0 else self.ring.at[kind - 1, o]
         return remote(
-            self.out.at[0, pb], self.relay.at[pb], self.ss.at[0, pb], self.rrs.at[pb],
-            self.along(True, step),
-        )
-
-    def ring_copy(self, d, pb):
+            self.out.at[kind, o], target, self.ss.at[kind, o], self.rs.at[kind, o],
+            self.along(True, 1 + 2 * side),
+        )
+
+    def send_relay(self, o):
+        self.out[0, o] = self.product(2, o).astype(BF16)
+        self.copy(0, o).start()
+
+    def send_fresh(self, o):
+        self.out[1, o] = self.product(3 - 2 * lax.rem(o, 2), o).astype(BF16)
+        self.copy(1, o).start()
+
+    def send_joined(self, o):
+        value = self.product(1 + 2 * lax.rem(o, 2), o)
+        self.copy(0, o).wait_recv()
+        self.out[2, o] = (value + self.relay[o].astype(F32)).astype(BF16)
+        self.copy(2, o).start()
+
+    def keep(self, o):
+        self.mine[o] = self.product(0, o)
+
+    def total(self, o):
+        for kind in (1, 2):
+            self.copy(kind, o).wait_recv()
+        return self.mine[o] + self.ring[0, o].astype(F32) + self.ring[1, o].astype(F32)
+
+    def halves(self, which):
         return remote(
-            self.out.at[1 + d, pb], self.ring.at[d, pb], self.ss.at[1 + d, pb], self.rs.at[d, pb],
-            self.along(True, 1 + 2 * d),
-        )
-
-    def send_relay(self):
-        def one(pb, carry):
-            self.out[0, pb] = self.product(lax.rem(self.ia + 2, 4), pb).astype(BF16)
-            self.relay_copy(pb).start()
-            return carry
-
-        lax.fori_loop(0, 4, one, 0)
-
-    def send_fresh(self):
-        def one(t, carry):
-            d = lax.div(t, 2)
-            pb = lax.rem(t + 2, 4)
-            self.out[1 + d, pb] = self.product(lax.rem(self.ia + 1 + 2 * d, 4), pb).astype(BF16)
-            self.ring_copy(d, pb).start()
-            return carry
-
-        lax.fori_loop(0, 4, one, 0)
-
-    def send_joined(self):
-        def one(pb, carry):
-            d = lax.div(pb, 2)
-            value = self.product(lax.rem(self.ia + 1 + 2 * d, 4), pb)
-            self.relay_copy(pb).wait_recv()
-            self.out[1 + d, pb] = (value + self.relay[pb].astype(F32)).astype(BF16)
-            self.ring_copy(d, pb).start()
-            return carry
-
-        lax.fori_loop(0, 4, one, 0)
-
-    def keep(self):
-        def one(pb, carry):
-            self.mine[pb] = self.product(self.ia, pb)
-            return carry
-
-        lax.fori_loop(0, 4, one, 0)
-
-    def halves(self, which):
-        place = lax.rem(self.ib + 2, 4)
-        rows = pl.ds(256 * which, 256)
-        return remote(
-            self.q.at[place, rows, :], self.relay2.at[which], self.ss2.at[which],
+            self.q.at[1, pl.ds(128 * which, 128), :], self.relay2.at[which], self.ss2.at[which],
             self.rs2.at[which], self.along(False, 1 + 2 * which),
         )
 
     def ends(self, which):
         return remote(
-            self.q.at[lax.rem(self.ib + 1 + 2 * which, 4)], self.ring2.at[which],
+            self.q.at[2 * which], self.ring2.at[which],
             self.ss2.at[2 + which], self.rs2.at[2 + which], self.along(False, 1 + 2 * which),
         )
 
     def turn(self):
-        def one(t, carry):
-            pb = lax.rem(self.ib + 2 + t, 4)
-            for d in (0, 1):
-                self.ring_copy(d, pb).wait_recv()
-            total = self.mine[pb] + self.ring[0, pb].astype(F32) + self.ring[1, pb].astype(F32)
-            self.mine[pb] = total
-            self.q[pb] = total.astype(BF16)
-            return carry
-
-        one(0, 0)
+        self.q[1] = self.total(2).astype(BF16)
         for which in (0, 1):
             self.halves(which).start()
-        lax.fori_loop(1, 4, one, 0)
 
     def join(self):
         for which in (0, 1):
+            value = self.total(1 + 2 * which)
             self.halves(which).wait_recv()
-            place = lax.rem(self.ib + 1 + 2 * which, 4)
-            rows = pl.ds(256 * which, 256)
-            self.q[place, rows, :] = (
-                self.mine[place, rows, :] + self.relay2[which].astype(F32)
-            ).astype(BF16)
+            met = pl.ds(128 * which, 128)
+            rest = slice(128, 256) if which == 0 else slice(0, 128)
+            same = slice(0, 128) if which == 0 else slice(128, 256)
+            self.q[2 * which, met, :] = (value[same] + self.relay2[which].astype(F32)).astype(BF16)
+            self.q[2 * which, pl.ds(128 - 128 * which, 128), :] = value[rest].astype(BF16)
             self.ends(which).start()
 
     def finish(self, result):
+        value = self.total(0)
         for which in (0, 1):
             self.ends(which).wait_recv()
-        result[...] = self.mine[self.ib] + self.ring2[0].astype(F32) + self.ring2[1].astype(F32)
+        result[self.rows, :] = value + self.ring2[0].astype(F32) + self.ring2[1].astype(F32)
 
     def drain(self):
-        def one(pb, carry):
-            self.relay_copy(pb).wait_send()
-            for d in (0, 1):
-                self.ring_copy(d, pb).wait_send()
+        def one(o, carry):
+            for kind in range(3):
+                self.copy(kind, o).wait_send()
             return carry
 
         lax.fori_loop(0, 4, one, 0)
         for which in (0, 1):
             self.halves(which).wait_send()
             self.ends(which).wait_send()
+
+
+class WeightSums:
+    def __init__(self, *sums):
+        self.sums = sums
+
+    def over(self, low, high, distance_of, names):
+        def one(t, carry):
+            for name in names:
+                for one_sum in self.sums:
+                    getattr(one_sum, name)(distance_of(t))
+            return carry
+
+        lax.fori_loop(low, high, one, 0)
+
+    def relay(self):
+        self.over(2, 6, lambda t: lax.rem(t, 4), ("send_relay",))
+
+    def fresh(self):
+        self.over(2, 4, lambda t: t, ("send_fresh",))
+
+    def joined(self):
+        self.over(2, 4, lambda t: t, ("send_joined",))
+
+    def others(self):
+        self.over(0, 2, lambda t: 1 - t, ("send_fresh", "send_joined"))
+
+    def keep(self):
+        self.over(0, 4, lambda t: t, ("keep",))
+
+    def turn(self):
+        for one_sum in self.sums:
+            one_sum.turn()
+
+    def join(self):
+        for one_sum in self.sums:
+            one_sum.join()
+
+    def finish(self, result):
+        for one_sum in self.sums:
+            one_sum.finish(result)
+
+    def drain(self):
+        for one_sum in self.sums:
+            one_sum.drain()
 
 
 class RowSum:
@@ -353,67 +404,59 @@
 
 
 class GateSum:
-    def __init__(self, place, parts, row, mid, col, total, send_sem, recv_sem):
+    def __init__(self, place, parts, row, total, send_sem, recv_sem):
         self.p = place
-        self.parts, self.row, self.mid, self.col, self.total = parts, row, mid, col, total
+        self.parts, self.row, self.total = parts, row, total
         self.ss, self.rs = send_sem, recv_sem
-
-    def copies(self, which, arriving):
-        p = self.p
-        if which == 4:
-            view = self.total.at[1 - p.k if arriving else p.k]
-            return [remote(view, view, self.ss.at[4, 0], self.rs.at[4, 0], p.other_core())]
-        found = []
-        for o in (1, 2, 3):
-            x, y = lax.rem(p.x + o, 4), lax.rem(p.y + o, 4)
-            back_x, back_y = lax.rem(p.x + 4 - o, 4), lax.rem(p.y + 4 - o, 4)
-            sems = self.ss.at[which, o - 1], self.rs.at[which, o - 1]
-            if which == 0:
-                src = self.parts.at[:, pl.ds(pl.multiple_of(x * 64, 64), 64), :]
-                dst = self.row.at[back_x if arriving else p.x]
-                found.append(remote(src, dst, *sems, p.along_x(o)))
-            elif which == 1:
-                src = self.mid.at[:, pl.ds(pl.multiple_of(y * 16, 16), 16), :]
-                dst = self.col.at[back_y if arriving else p.y]
-                found.append(remote(src, dst, *sems, p.along_y(o)))
-            elif which == 2:
-                at = p.x * 64 + (back_y if arriving else p.y) * 16
-                view = self.total.at[p.k, :, pl.ds(pl.multiple_of(at, 16), 16), :]
-                found.append(remote(view, view, *sems, p.along_y(o)))
-            else:
-                at = (back_x if arriving else p.x) * 64
-                view = self.total.at[p.k, :, pl.ds(pl.multiple_of(at, 64), 64), :]
-                found.append(remote(view, view, *sems, p.along_x(o)))
-        return found
+        self.chip = lax.div(place.c, 2)
+        view = total.at[place.k]
+        self.pair = remote(view, view, send_sem.at[2, 0], recv_sem.at[2, 0], place.other_core())
+
+    def rows(self, chip):
+        return pl.ds(pl.multiple_of(chip * 16, 16), 16)
+
+    def copy(self, which, o, arriving):
+        owner = lax.rem(self.chip + 16 - o, 16) if arriving else self.chip
+        peer = lax.rem(self.chip + o, 16)
+        if which == 0:
+            src, dst = self.parts.at[:, self.rows(peer), :], self.row.at[owner]
+        else:
+            src = dst = self.total.at[self.p.k, :, self.rows(owner), :]
+        return remote(
+            src, dst, self.ss.at[which, o], self.rs.at[which, o], (peer * 2 + self.p.k, self.p.m)
+        )
+
+    def each(self, act):
+        def one(o, carry):
+            act(o)
+            return carry
+
+        lax.fori_loop(1, 16, one, 0)
 
     def start(self, which):
-        p = self.p
+        if which == 2:
+            self.pair.start()
+            return
         if which == 0:
-            mine = pl.ds(pl.multiple_of(p.x * 64, 64), 64)
-            self.row[p.x] = self.parts[:, mine, :]
-        if which == 1:
+            self.row[self.chip] = self.parts[:, self.rows(self.chip), :]
+        else:
             total = self.row[0].astype(F32)
-            for o in (1, 2, 3):
+            for o in range(1, 16):
                 total = total + self.row[o].astype(F32)
-            self.mid[...] = total.astype(BF16)
-            self.col[p.y] = self.mid[:, pl.ds(pl.multiple_of(p.y * 16, 16), 16), :]
+            self.total[self.p.k, :, self.rows(self.chip), :] = total.astype(BF16)
+        self.each(lambda o: self.copy(which, o, False).start())
+
+    def finish(self, which):
         if which == 2:
-            total = self.col[0].astype(F32)
-            for o in (1, 2, 3):
-                total = total + self.col[o].astype(F32)
-            at = pl.ds(pl.multiple_of(p.x * 64 + p.y * 16, 16), 16)
-            self.total[p.k, :, at, :] = total.astype(BF16)
-        for copy in self.copies(which, False):
-            copy.start()
-
-    def finish(self, which):
-        for copy in self.copies(which, True):
-            copy.wait_recv()
+            view = self.total.at[1 - self.p.k]
+            remote(view, view, self.ss.at[2, 0], self.rs.at[2, 0], self.p.other_core()).wait_recv()
+        else:
+            self.each(lambda o: self.copy(which, o, True).wait_recv())
 
     def drain(self):
-        for which in range(5):
-            for copy in self.copies(which, False):
-                copy.wait_send()
+        for which in (0, 1):
+            self.each(lambda o: self.copy(which, o, False).wait_send())
+        self.pair.wait_send()
 
 
 def minus_expm1(v):
@@ -431,34 +474,37 @@
 
 
 def first_kernel(
-    tokens, branch, out_grad, w_in, conv_w, gate_a, gate_a_b, gate_i, gate_i_b, decay_param, w_out,
+    tokens, branch, out_grad, w_in, conv_w, gate_a_h, gate_a_b, gate_i_h, gate_i_b, decay_param, w_out,
     state_init, conv_history,
     tokens_grad, branch_grad, w_in_t, w_out_grad, small, gate_total,
-    tok, og, proj, gated, conv_b, ri, tok_o, og_o, conv_o, ri_o, gate_p, gate_row, gate_mid, gate_col,
-    lhs_g, lhs_p, parts, came,
+    tok, og, proj, gated, conv_b, ri, tok_o, og_o, conv_o, ri_o, gate_p, gate_row,
+    lhs_g, lhs_p, parts, came, branch_v, gate_a, gate_i,
     w_in_v, w_out_v, acc, px, cv, rg, ig, dk, rem, hs, cp, ep, br, gp, cg, kv, edge_s, edge_r, edge_c,
-    core_s, row_s, col_s, core_b, row_b, col_b,
-    core_m, row_m, col_m,
+    all_s, all_b, core_m, row_m, col_m,
     w_sem, ts, tr, gs, gr, fs, fr, bs, brs, es, er, ms, mr, zs, zr, ps, pr, qs, qr,
     *sums,
 ):
     p = Place()
     loads = [
-        pltpu.make_async_copy(w_in, w_in_v, w_sem.at[0]),
-        pltpu.make_async_copy(w_out, w_out_v, w_sem.at[1]),
+        pltpu.make_async_copy(src, dst, w_sem.at[n])
+        for n, (src, dst) in enumerate(
+            (
+                (tokens, tok.at[p.m]),
+                (out_grad, og.at[p.m]),
+                (branch, branch_v),
+                (gate_a_h, gate_a),
+                (gate_i_h, gate_i),
+                (w_in, w_in_v),
+                (w_out, w_out_v),
+            )
+        )
     ]
     for load in loads:
         load.start()
-    tok[p.m] = tokens[...]
-    og[p.m] = out_grad[...]
-    enter(
-        p,
-        [p.along_z(1), p.along_z(NMP - 1), p.along_ctx(1), p.along_ctx(31), p.other_core()]
-        + [p.along_x(o) for o in (1, 2, 3)]
-        + [p.along_y(o) for o in (1, 2, 3)],
-    )
+    enter(p, [p.along_z(1), p.along_z(NMP - 1)] + [p.along_ctx(o) for o in range(1, 32)])
     tokens_in = Gather(p, tok, ts, tr)
     grads_in = Gather(p, og, gs, gr)
+    loads[0].wait()
     tokens_in.send(0)
 
     def wide(row):
@@ -477,12 +523,17 @@
         gap == 0.0, small_exp, jnp.log(one_more) * (small_exp / jnp.where(gap == 0.0, 1.0, gap))
     )
     kv[6] = jnp.maximum(negative, 0.0) + log_part
-    br[...] = to_segments(branch[...].astype(F32))
-
-    for s in (0, 1, 2):
-        tokens_in.arrive(s)
+    loads[1].wait()
+    loads[2].wait()
+    br[...] = to_segments(branch_v[...].astype(F32))
+
+    tokens_in.arrive(0)
     grads_in.send(0)
-    loads[0].wait()
+    for load in loads[3:]:
+        load.wait()
+    tokens_in.arrive(1)
+    tokens_in.arrive(2)
+    grads_in.arrive(0)
     tokens_in.arrive(3)
     other_tokens = CoreColumns(p, tok, tok_o, ps.at[0], pr.at[0])
     other_grads = CoreColumns(p, og, og_o, ps.at[1], pr.at[1])
@@ -491,10 +542,16 @@
     other_proj = CorePair(p, lhs_p.at[0], lhs_p.at[1], ps.at[4], pr.at[4])
     other_gate = CorePair(p, ri.at[1 - p.k], ri_o, ps.at[5], pr.at[5])
     pairs = [other_tokens, other_grads, other_conv, other_gated, other_proj, other_gate]
-    w_out_sum = WeightSum(p, False, lhs_g, og, og_o, sums[:12])
-    w_in_sum = WeightSum(p, True, lhs_p, tok, tok_o, sums[12:])
+    w_out_sum = WeightSums(
+        WeightSum(p, True, lhs_g, og, og_o, sums[:11]),
+        WeightSum(p, False, lhs_g, og, og_o, sums[11:22]),
+    )
+    w_in_sum = WeightSums(
+        WeightSum(p, True, lhs_p, tok, tok_o, sums[22:33]),
+        WeightSum(p, False, lhs_p, tok, tok_o, sums[33:]),
+    )
     row_sum = RowSum(p, parts, came, zs, zr)
-    gate_sum = GateSum(p, gate_p, gate_row, gate_mid, gate_col, gate_total, qs, qr)
+    gate_sum = GateSum(p, gate_p, gate_row, gate_total, qs, qr)
     total_sum = Fold(p, core_m, row_m, col_m, ms, mr)
     other_tokens.start()
 
@@ -512,7 +569,6 @@
     forward_edge = remote(edge_s, edge_r, es.at[0], er.at[0], p.along_ctx(1))
     forward_edge.start()
     px[pl.ds(3, 32)] = to_segments(acc[...].astype(BF16).astype(F32))
-    grads_in.arrive(0)
 
     lane8 = lax.broadcasted_iota(jnp.int32, (8, CH), 0)
     forward_edge.wait_recv()
@@ -573,14 +629,8 @@
         )
     c_before = jnp.where(lane8 == 0, 1.0, pltpu.roll(c, 1, 0))
     h_before = jnp.where(lane8 == 0, 0.0, pltpu.roll(h, 1, 0))
-    states = Fold(p, core_s, row_s, col_s, fs, fr)
-    pair = jnp.where(lane8 < 4, wide(c[7:8]), wide(h[7:8]))
-
-    def both(slot):
-        value = slot
-        return wide(value[0:1]), wide(value[4:5])
-
-    states.start(0, pair)
+    states = Everyone(p, all_s, fs, fr)
+    states.start(jnp.concatenate([c[7:8], h[7:8]], 0))
     grads_in.arrive(1)
 
     def suffix(n, e):
@@ -588,25 +638,12 @@
         return e * dk[31 - n]
 
     lax.fori_loop(0, 32, suffix, jnp.ones((8, CH), F32))
-    states.finish(0)
-    c0, h0 = both(core_s[0])
-    c1, h1 = both(core_s[1])
-    states.start(1, jnp.where(lane8 < 4, c0 * c1, c1 * h0 + h1))
-    states.finish(1)
-    cr, hr = jnp.ones((8, CH), F32), jnp.zeros((8, CH), F32)
-    for o in range(4):
-        co, ho = both(row_s[o])
-        cr, hr = cr * co, co * hr + ho
-    states.start(2, jnp.where(lane8 < 4, cr, hr))
-    states.finish(2)
-    state = wide(state_init[...])
-    for o in range(4):
-        co, ho = both(col_s[o])
-        state = jnp.where(o < p.y, co * state + ho, state)
-    for o in range(4):
-        co, ho = both(row_s[o])
-        state = jnp.where(o < p.x, co * state + ho, state)
-    state = jnp.where(p.k == 1, c0 * state + h0, state)
+    states.finish()
+    state = state_init[...].reshape(1, CH)
+    for o in range(32):
+        one = all_s[o]
+        state = jnp.where(o < p.c, one[0:1] * state + one[1:2], state)
+    state = wide(state)
     seg_state = h_before + c_before * state
     hs[0] = seg_state
 
@@ -623,7 +660,6 @@
     other_gated.start()
 
     grads_in.arrive(2)
-    loads[1].wait()
     grads_in.arrive(3)
     other_grads.start()
     acc[...] = jnp.zeros_like(acc)
@@ -654,28 +690,18 @@
         )
     c_after = jnp.where(lane8 == 7, 1.0, pltpu.roll(c, 7, 0))
     b_after = jnp.where(lane8 == 7, 0.0, pltpu.roll(b, 7, 0))
-    adjoints = Fold(p, core_b, row_b, col_b, bs, brs)
-    adjoints.start(0, wide(b[0:1]))
+    adjoints = Everyone(p, all_b, bs, brs)
+    adjoints.start(b[0:1])
     other_gated.finish()
     other_grads.finish()
-    w_out_sum.send_relay()
-    adjoints.finish(0)
-    b0, b1 = core_b[0], core_b[1]
-    adjoints.start(1, b0 + c0 * b1)
-    w_out_sum.send_fresh()
-    adjoints.finish(1)
-    row = jnp.zeros((8, CH), F32)
-    for o in (3, 2, 1, 0):
-        row = row_b[o] + both(row_s[o])[0] * row
-    adjoints.start(2, row)
+    w_out_sum.relay()
     branch_grad[...] = from_segments(cp[...]).astype(BF16)
-    adjoints.finish(2)
-    later = jnp.zeros((8, CH), F32)
-    for o in (3, 2, 1, 0):
-        later = jnp.where(o > p.y, col_b[o] + both(col_s[o])[0] * later, later)
-    for o in (3, 2, 1, 0):
-        later = jnp.where(o > p.x, row_b[o] + both(row_s[o])[0] * later, later)
-    later = jnp.where(p.k == 0, b1 + c1 * later, later)
+    w_out_sum.fresh()
+    adjoints.finish()
+    later = jnp.zeros((1, CH), F32)
+    for o in reversed(range(32)):
+        later = jnp.where(o > p.c, all_b[o] + all_s[o][0:1] * later, later)
+    later = wide(later)
     seg_later = b_after + c_after * later
 
     def gate_grads(n, carry):
@@ -710,7 +736,9 @@
         ).reshape(32, 8, 256)
     backward_edge = remote(cg.at[pl.ds(0, 3)], edge_c, es.at[1], er.at[1], p.along_ctx(31))
     backward_edge.start()
-    w_out_sum.send_joined()
+    w_out_sum.joined()
+    w_out_sum.others()
+    w_out_sum.keep()
     backward_edge.wait_recv()
     for j in range(3):
         turned = pltpu.roll(cg[j], 7, 0)
@@ -743,11 +771,6 @@
         row_sum.begin(part)
     rows = [jnp.sum(v, 0, keepdims=True) for v in (*tap_sums, sum_r, sum_a, sum_i)]
     total_sum.start(0, jnp.concatenate(rows + [jnp.zeros((1, CH), F32)], 0))
-    other_tokens.finish()
-    other_proj.finish()
-    w_in_sum.send_relay()
-    w_in_sum.send_fresh()
-    row_sum.step(1)
     other_conv.finish()
     other_gate.finish()
     for b in (0, 1):
@@ -756,33 +779,34 @@
             matmul_tn(conv_b[:, cols], ri[p.k, :, cols]) + matmul_tn(conv_o[:, cols], ri_o[:, cols])
         ).astype(BF16)
     gate_sum.start(0)
-    w_out_sum.keep()
+    other_tokens.finish()
+    other_proj.finish()
+    w_in_sum.relay()
+    w_in_sum.fresh()
+    row_sum.step(1)
     w_out_sum.turn()
-    w_in_sum.send_joined()
+    w_in_sum.joined()
+    w_in_sum.others()
     row_sum.step(2)
-    total_sum.finish(0)
-    total_sum.start(1, core_m[0] + core_m[1])
+    w_in_sum.keep()
     gate_sum.finish(0)
     gate_sum.start(1)
     w_out_sum.join()
-    w_in_sum.keep()
+    total_sum.finish(0)
+    total_sum.start(1, core_m[0] + core_m[1])
+    w_in_sum.turn()
     row_sum.step(3)
+    w_in_sum.join()
+    gate_sum.finish(1)
+    gate_sum.start(2)
     total_sum.finish(1)
     total_sum.start(2, row_m[0] + row_m[1] + row_m[2] + row_m[3])
-    w_in_sum.turn()
-    gate_sum.finish(1)
-    gate_sum.start(2)
     w_out_sum.finish(w_out_grad)
-    gate_sum.finish(2)
-    gate_sum.start(3)
-    w_in_sum.join()
+    w_in_sum.finish(w_in_t)
     total_sum.finish(2)
     small[...] = col_m[0] + col_m[1] + col_m[2] + col_m[3]
-    gate_sum.finish(3)
-    gate_sum.start(4)
     row_sum.finish(tokens_grad)
-    w_in_sum.finish(w_in_t)
-    gate_sum.finish(4)
+    gate_sum.finish(2)
     for used in (states, adjoints, total_sum, w_out_sum, w_in_sum, row_sum, gate_sum, *pairs):
         used.drain()
     tokens_in.sent()
@@ -808,20 +832,19 @@
         S((2, 2, 256, 256), BF16),
     )
     weight = [
-        vm((3, 4, CH, 128), BF16),
-        vm((4, CH, 128), F32),
-        vm((4, CH, 128), BF16),
-        vm((2, 4, CH, 128), BF16),
-        vm((4, CH, 128), BF16),
+        vm((3, 4, 256, 128), BF16),
+        vm((4, 256, 128), F32),
+        vm((4, 256, 128), BF16),
+        vm((2, 4, 256, 128), BF16),
+        vm((3, 256, 128), BF16),
+        vm((2, 128, 128), BF16),
         vm((2, 256, 128), BF16),
-        vm((2, CH, 128), BF16),
         dma((3, 4)),
-        dma((4,)),
-        dma((2, 4)),
+        dma((3, 4)),
         dma((4,)),
         dma((4,)),
     ]
-    big = {3, 10}
+    big = {0, 1, 2, 3, 5, 7, 10}
     return pl.pallas_call(
         first_kernel,
         out_shape=outs,
@@ -841,13 +864,14 @@
             vm((256, CH), BF16),
             vm((256, CH), BF16),
             vm((2, 256, 256), BF16),
-            vm((4, 2, 64, 256), BF16),
-            vm((2, 64, 256), BF16),
-            vm((4, 2, 16, 256), BF16),
+            vm((16, 2, 16, 256), BF16),
             vm((2, CH, 256), BF16),
             vm((2, CH, 256), BF16),
             vm((8, 32, DM), BF16),
             vm((2, 4, 32, DM), BF16),
+            vm((256, CH), BF16),
+            vm((2, 256, 256), BF16),
+            vm((2, 256, 256), BF16),
             vm((DM, CH), BF16),
             vm((CH, DM), BF16),
             vm((256, CH), F32),
@@ -860,24 +884,20 @@
             vm((16, CH), BF16),
             vm((16, CH), BF16),
             vm((3, 8, CH), F32),
+            vm((32, 2, CH), F32),
+            vm((32, 1, CH), F32),
             vm((2, *tile), F32),
             vm((4, *tile), F32),
             vm((4, *tile), F32),
-            vm((2, *tile), F32),
-            vm((4, *tile), F32),
-            vm((4, *tile), F32),
-            vm((2, *tile), F32),
-            vm((4, *tile), F32),
-            vm((4, *tile), F32),
-            dma((2,)),
+            dma((7,)),
             dma((2, 4, 2)),
             dma((2, 4, 2)),
             dma((2, 4, 2)),
             dma((2, 4, 2)),
-            dma((7,)),
-            dma((7,)),
-            dma((7,)),
-            dma((7,)),
+            dma((32,)),
+            dma((32,)),
+            dma((32,)),
+            dma((32,)),
             dma((2,)),
             dma((2,)),
             dma((7,)),
@@ -886,8 +906,10 @@
             dma((2, 4, 2)),
             dma((6,)),
             dma((6,)),
-            dma((5, 3)),
-            dma((5, 3)),
+            dma((3, 16)),
+            dma((3, 16)),
+            *weight,
+            *weight,
             *weight,
             *weight,
         ],

time: 129 us -> 112 us (0.87)
  Pallas kernels: 128 us -> 110 us
    pallas_call x1, Pallas kernels: 126 us -> 108 us  [call_first(): pl.pallas_call(first_kernel, out_shape=outs, in_specs=[pl.BlockSpec(memor...]
where the time goes in v3:
time: 112 us; the launch traced here: 111 us
  Pallas kernels  110 us (98%)
    pallas_call x1, Pallas kernels, call_first(): pl.pallas_call(first_kernel, out_shape=outs, in_specs=[pl.BlockSpec(memor...  108 us
    pallas_call x1, Pallas kernels, shards(): pl.pallas_call(last_kernel, out_shape=outs, in_specs=[pl.BlockSpec(memory...  2.77 us

profile of v3, /device:TPU:1, one launch (start us, length us, event | category | flops | bytes accessed | tf_op | source)
XLA Modules:
  0.0 111.0 jit_solution(8866685857491385406)
XLA Ops:
  0.6 107.6 %shard_map.204 = (bf16[32,4096]{1,0:T(8,128)(2,1)}, bf16[256,512]{1,0:T(8,128)(2,1)}, f32[512,128]{1,0:T(8,128)}, f32[512,128]{1,0:T(8,128)}, f32[8,512]{1,0:T(8,128)}, /*index=5*/bf16[2,2,256,256]{3,2,1,0:T(8,128)(2,1)}) custom-call(bf16[32,4096]{1,0:T(8,128)(2,1)} %tokens.1, bf16[256,512]{1,0:T(8,128)(2,1)} %branch.1, bf16[32,4096]{1,0:T(8,128)(2,1)} %out_grad.1, ...), custom_call_target="tpu_custom_call" | custom-call | tf_op jit(solution)/shard_map/pallas_call | solution.py:848
  108.3 2.8 %shard_map.205 = (bf16[32,4096]{1,0:T(8,128)(2,1)}, bf16[256,512]{1,0:T(8,128)(2,1)}, f32[128,512]{1,0:T(8,128)}, f32[512,128]{1,0:T(8,128)}, f32[4,512]{1,0:T(4...) custom-call(bf16[32,4096]{1,0:T(8,128)(2,1)} %get-tuple-element.16.tokens_, ...), custom_call_target="tpu_custom_call" | custom-call | tf_op jit(solution)/shard_map/pallas_call | solution.py:954

commit v4 on v3

--- a/solution.py
+++ b/solution.py
@@ -152,11 +152,11 @@
     def start(self, value):
         self.slots[self.p.c] = value
 
-        def one(o, carry):
-            self.copy(o, self.p.c).start()
+        def one(t, carry):
+            self.copy(1 + lax.rem(t + 17, 31), self.p.c).start()
             return carry
 
-        lax.fori_loop(1, 32, one, 0)
+        lax.fori_loop(0, 31, one, 0)
 
     def finish(self):
         def one(o, carry):
@@ -218,18 +218,26 @@
     def along(self, first, step):
         return self.p.along_x(step) if first == self.first_x else self.p.along_y(step)
 
-    def product(self, distance, o):
+    def columns(self, distance, o):
         pa, pb = lax.rem(self.ia + distance, 4), lax.rem(self.ib + o, 4)
         j = pb * 4 + pa if self.first_x else pa * 4 + pb
         here = pl.ds(pl.multiple_of((2 * j + self.p.k) * 128, 128), 128)
         there = pl.ds(pl.multiple_of(j * 128, 128), 128)
-        return jnp.dot(
-            self.lhs[0, self.rows, :], self.own[:, :, here].reshape(256, 128),
-            preferred_element_type=F32,
-        ) + jnp.dot(
-            self.lhs[1, self.rows, :], self.other[:, :, there].reshape(256, 128),
-            preferred_element_type=F32,
-        )
+        return (
+            self.own[:, :, here].reshape(256, 128), self.other[:, :, there].reshape(256, 128)
+        )
+
+    def products(self, one, two):
+        one, two = self.columns(*one), self.columns(*two)
+        both = [
+            jnp.dot(
+                self.lhs[n, self.rows, :], jnp.concatenate([one[n], two[n]], 1),
+                preferred_element_type=F32,
+            )
+            for n in (0, 1)
+        ]
+        both = both[0] + both[1]
+        return both[:, :128], both[:, 128:]
 
     def copy(self, kind, o):
         side = lax.rem(o, 2) if kind != 1 else 1 - lax.rem(o, 2)
@@ -240,21 +248,36 @@
         )
 
     def send_relay(self, o):
-        self.out[0, o] = self.product(2, o).astype(BF16)
-        self.copy(0, o).start()
-
-    def send_fresh(self, o):
-        self.out[1, o] = self.product(3 - 2 * lax.rem(o, 2), o).astype(BF16)
+        for n, value in enumerate(self.products((2, o), (2, o + 1))):
+            self.out[0, o + n] = value.astype(BF16)
+            self.copy(0, o + n).start()
+
+    def fresh(self, o, value):
+        self.out[1, o] = value.astype(BF16)
         self.copy(1, o).start()
 
-    def send_joined(self, o):
-        value = self.product(1 + 2 * lax.rem(o, 2), o)
+    def joined(self, o, value):
         self.copy(0, o).wait_recv()
         self.out[2, o] = (value + self.relay[o].astype(F32)).astype(BF16)
         self.copy(2, o).start()
 
+    def send_fresh(self):
+        for o, value in zip((3, 2), self.products((1, 3), (3, 2))):
+            self.fresh(o, value)
+
+    def send_joined(self):
+        for o, value in zip((2, 3), self.products((1, 2), (3, 3))):
+            self.joined(o, value)
+
+    def send_others(self, o):
+        far = 2 * lax.rem(o, 2)
+        values = self.products((3 - far, o), (1 + far, o))
+        self.fresh(o, values[0])
+        self.joined(o, values[1])
+
     def keep(self, o):
-        self.mine[o] = self.product(0, o)
+        for n, value in enumerate(self.products((0, o), (0, o + 1))):
+            self.mine[o + n] = value
 
     def total(self, o):
         for kind in (1, 2):
@@ -289,11 +312,15 @@
             self.q[2 * which, pl.ds(128 - 128 * which, 128), :] = value[rest].astype(BF16)
             self.ends(which).start()
 
-    def finish(self, result):
+    def finish(self, result, turned):
         value = self.total(0)
         for which in (0, 1):
             self.ends(which).wait_recv()
-        result[self.rows, :] = value + self.ring2[0].astype(F32) + self.ring2[1].astype(F32)
+        value = value + self.ring2[0].astype(F32) + self.ring2[1].astype(F32)
+        if turned:
+            result[:, self.rows] = value.T
+        else:
+            result[self.rows, :] = value
 
     def drain(self):
         def one(o, carry):
@@ -311,29 +338,30 @@
     def __init__(self, *sums):
         self.sums = sums
 
-    def over(self, low, high, distance_of, names):
+    def twice(self, name, of):
         def one(t, carry):
-            for name in names:
-                for one_sum in self.sums:
-                    getattr(one_sum, name)(distance_of(t))
+            for one_sum in self.sums:
+                getattr(one_sum, name)(of(t))
             return carry
 
-        lax.fori_loop(low, high, one, 0)
+        lax.fori_loop(0, 2, one, 0)
 
     def relay(self):
-        self.over(2, 6, lambda t: lax.rem(t, 4), ("send_relay",))
+        self.twice("send_relay", lambda t: 2 - 2 * t)
 
     def fresh(self):
-        self.over(2, 4, lambda t: t, ("send_fresh",))
+        for one_sum in self.sums:
+            one_sum.send_fresh()
 
     def joined(self):
-        self.over(2, 4, lambda t: t, ("send_joined",))
+        for one_sum in self.sums:
+            one_sum.send_joined()
 
     def others(self):
-        self.over(0, 2, lambda t: 1 - t, ("send_fresh", "send_joined"))
+        self.twice("send_others", lambda t: 1 - t)
 
     def keep(self):
-        self.over(0, 4, lambda t: t, ("keep",))
+        self.twice("keep", lambda t: 2 * t)
 
     def turn(self):
         for one_sum in self.sums:
@@ -343,9 +371,9 @@
         for one_sum in self.sums:
             one_sum.join()
 
-    def finish(self, result):
+    def finish(self, result, turned):
         for one_sum in self.sums:
-            one_sum.finish(result)
+            one_sum.finish(result, turned)
 
     def drain(self):
         for one_sum in self.sums:
@@ -476,7 +504,9 @@
 def first_kernel(
     tokens, branch, out_grad, w_in, conv_w, gate_a_h, gate_a_b, gate_i_h, gate_i_b, decay_param, w_out,
     state_init, conv_history,
-    tokens_grad, branch_grad, w_in_t, w_out_grad, small, gate_total,
+    tokens_grad, branch_grad, w_in_grad, w_out_grad, conv_grad, gate_a_grad, bias_a_grad, gate_i_grad,
+    bias_i_grad, decay_grad,
+    gate_total, w_in_t, w_out_t, pieces,
     tok, og, proj, gated, conv_b, ri, tok_o, og_o, conv_o, ri_o, gate_p, gate_row,
     lhs_g, lhs_p, parts, came, branch_v, gate_a, gate_i,
     w_in_v, w_out_v, acc, px, cv, rg, ig, dk, rem, hs, cp, ep, br, gp, cg, kv, edge_s, edge_r, edge_c,
@@ -532,7 +562,16 @@
     for load in loads[3:]:
         load.wait()
     tokens_in.arrive(1)
+
+    def turn_weights(n, carry):
+        at = pl.ds(pl.multiple_of(n * 512, 512), 512)
+        w_out_t[at, :] = w_out_v[:, at].T
+        w_in_t[:, at] = w_in_v[at, :].T
+        return carry
+
+    lax.fori_loop(0, 4, turn_weights, 0)
     tokens_in.arrive(2)
+    lax.fori_loop(4, 8, turn_weights, 0)
     grads_in.arrive(0)
     tokens_in.arrive(3)
     other_tokens = CoreColumns(p, tok, tok_o, ps.at[0], pr.at[0])
@@ -558,13 +597,13 @@
     acc[...] = jnp.zeros_like(acc)
 
     def project(n, carry):
-        at = pl.ds(pl.multiple_of(n * 512, 512), 512)
+        at = pl.ds(pl.multiple_of(n * 1024, 1024), 1024)
         acc[...] += jnp.dot(
-            tok[:, :, at].reshape(256, 512), w_in_v[at, :], preferred_element_type=F32
+            tok[:, :, at].reshape(256, 1024), w_in_v[at, :], preferred_element_type=F32
         )
         return carry
 
-    lax.fori_loop(0, 8, project, 0)
+    lax.fori_loop(0, 4, project, 0)
     edge_s[...] = acc[pl.ds(240, 16), :].astype(BF16)
     forward_edge = remote(edge_s, edge_r, es.at[0], er.at[0], p.along_ctx(1))
     forward_edge.start()
@@ -659,17 +698,48 @@
     lhs_g[0] = gated[...].T
     other_gated.start()
 
+    def coefficients(n, carry):
+        at = pl.ds(2 * n, 2)
+        decay, remain, inp, recur, wide_conv = dk[at], rem[at], ig[at], rg[at], cv[at]
+        scaler = jnp.sqrt(remain)
+        inner = inp * wide_conv
+        log_part = hs[at] * decay - 2.0 * decay * decay * inner / jnp.sqrt(
+            jnp.maximum(4.0 * remain, 1e-06)
+        )
+        rate_part = -8.0 * recur * log_part
+        rem[at] = scaler * inp
+        ig[at] = inner * scaler * (1.0 - inp)
+        rg[at] = rate_part
+        cv[at] = rate_part * kv[6] * (1.0 - recur)
+        return carry
+
+    lax.fori_loop(0, 16, coefficients, 0)
     grads_in.arrive(2)
+    there = (0, 1, 7, 2, 6, 3, 5)
+
+    def place_of(offset):
+        return lax.rem(p.m + offset, NMP)
+
+    def early_product(n, carry):
+        at = pl.ds(pl.multiple_of(n * 1024, 1024), 1024)
+        rows = jnp.concatenate([og[place_of(o), :, at] for o in there], 0)
+        value = jnp.dot(rows, w_out_t[at, :], preferred_element_type=F32).reshape(7, 32, CH)
+        pieces[pl.ds(0, 7)] = jnp.where(n == 0, value, pieces[pl.ds(0, 7)] + value)
+        return carry
+
+    def late_product(n, carry):
+        at = pl.ds(pl.multiple_of(n * 1024, 1024), 1024)
+        return carry + jnp.dot(og[place_of(4), :, at], w_out_t[at, :], preferred_element_type=F32)
+
+    pieces[...] = jnp.zeros_like(pieces)
+    lax.fori_loop(0, 4, early_product, 0)
+    for n, offset in enumerate(there):
+        acc[pl.ds(pl.multiple_of(place_of(offset) * 32, 32), 32), :] = pieces[n]
     grads_in.arrive(3)
     other_grads.start()
-    acc[...] = jnp.zeros_like(acc)
-
-    def grad_product(n, carry):
-        at = pl.ds(pl.multiple_of(n * 512, 512), 512)
-        acc[...] += matmul_nt(og[:, :, at].reshape(256, 512), w_out_v[:, at])
-        return carry
-
-    lax.fori_loop(0, 8, grad_product, 0)
+    acc[pl.ds(pl.multiple_of(place_of(4) * 32, 32), 32), :] = lax.fori_loop(
+        0, 4, late_product, jnp.zeros((32, CH), F32)
+    )
     gp[...] = to_segments(acc[...])
 
     def backward(n, b):
@@ -708,22 +778,16 @@
         sum_a, sum_i, sum_r = carry
         at = pl.ds(2 * n, 2)
         adjoint = gp[at] + ep[at] * seg_later
-        decay, remain, inp, recur, wide_conv = dk[at], rem[at], ig[at], rg[at], cv[at]
-        scaler = jnp.sqrt(remain)
-        scaler_grad = adjoint * inp * wide_conv
-        log_grad = adjoint * hs[at] * decay - 2.0 * decay * decay * scaler_grad / jnp.sqrt(
-            jnp.maximum(4.0 * remain, 1e-06)
-        )
-        recur_pre = (log_grad * (-8.0 * kv[6]) * recur * (1.0 - recur)).astype(BF16)
-        input_pre = (scaler_grad * scaler * (1.0 - inp)).astype(BF16)
+        recur_pre = (adjoint * cv[at]).astype(BF16)
+        input_pre = (adjoint * ig[at]).astype(BF16)
         flat = pl.ds(pl.multiple_of(16 * n, 16), 16)
         ri[0, flat, :] = recur_pre.reshape(16, CH)
         ri[1, flat, :] = input_pre.reshape(16, CH)
-        cg[at] = adjoint * scaler * inp
+        cg[at] = adjoint * rem[at]
         return (
             sum_a + jnp.sum(recur_pre.astype(F32), 0),
             sum_i + jnp.sum(input_pre.astype(F32), 0),
-            sum_r + jnp.sum(log_grad * (-8.0 * recur), 0),
+            sum_r + jnp.sum(adjoint * rg[at], 0),
         )
 
     zero = jnp.zeros((8, CH), F32)
@@ -764,7 +828,8 @@
 
         def spread(n, carry):
             at = pl.ds(pl.multiple_of(n * 512, 512), 512)
-            parts[:, :, at] = matmul_nt(proj[...], w_in_v[at, :]).astype(BF16).reshape(8, 32, 512)
+            value = jnp.dot(proj[...], w_in_t[:, at], preferred_element_type=F32)
+            parts[:, :, at] = value.astype(BF16).reshape(8, 32, 512)
             return carry
 
         lax.fori_loop(part * 4, part * 4 + 4, spread, 0)
@@ -801,12 +866,19 @@
     gate_sum.start(2)
     total_sum.finish(1)
     total_sum.start(2, row_m[0] + row_m[1] + row_m[2] + row_m[3])
-    w_out_sum.finish(w_out_grad)
-    w_in_sum.finish(w_in_t)
+    gates_out = (gate_a_grad, gate_i_grad)
+    w_out_sum.finish(w_out_grad, False)
+    w_in_sum.finish(w_in_grad, True)
     total_sum.finish(2)
-    small[...] = col_m[0] + col_m[1] + col_m[2] + col_m[3]
+    small = col_m[0] + col_m[1] + col_m[2] + col_m[3]
+    conv_grad[...] = small[0:4]
+    bias_a_grad[...] = small[5]
+    bias_i_grad[...] = small[6]
+    decay_grad[...] = small[4] * -jax.nn.sigmoid(-decay_param[...])
     row_sum.finish(tokens_grad)
     gate_sum.finish(2)
+    for n in (0, 1):
+        gates_out[n][...] = gate_total[n].astype(F32)
     for used in (states, adjoints, total_sum, w_out_sum, w_in_sum, row_sum, gate_sum, *pairs):
         used.drain()
     tokens_in.sent()
@@ -815,6 +887,24 @@
     backward_edge.wait_send()
 
 
+def result(shape, dtype):
+    return jax.ShapeDtypeStruct(shape, dtype)
+
+
+OUTS = (
+    result((32, DM), BF16),
+    result((256, CH), BF16),
+    result((128, CH), F32),
+    result((CH, 128), F32),
+    result((4, CH), F32),
+    result((2, 256, 256), F32),
+    result((CH,), F32),
+    result((2, 256, 256), F32),
+    result((CH,), F32),
+    result((CH,), F32),
+)
+
+
 def call_first(*args):
     def vm(shape, dtype):
         return pltpu.VMEM(shape, dtype)
@@ -822,15 +912,7 @@
     seg = (32, 8, CH)
     tile = (8, CH)
     dma = pltpu.SemaphoreType.DMA
-    S = jax.ShapeDtypeStruct
-    outs = (
-        S((32, DM), BF16),
-        S((256, CH), BF16),
-        S((CH, 128), F32),
-        S((CH, 128), F32),
-        S((8, CH), F32),
-        S((2, 2, 256, 256), BF16),
-    )
+    outs = OUTS
     weight = [
         vm((3, 4, 256, 128), BF16),
         vm((4, 256, 128), F32),
@@ -853,6 +935,10 @@
         ],
         out_specs=tuple(pl.BlockSpec(memory_space=pltpu.VMEM) for _ in outs),
         scratch_shapes=[
+            vm((2, 2, 256, 256), BF16),
+            vm((CH, DM), BF16),
+            vm((DM, CH), BF16),
+            vm((8, 32, CH), F32),
             vm((8, 32, DM), BF16),
             vm((8, 32, DM), BF16),
             vm((256, CH), BF16),
@@ -919,44 +1005,23 @@
     )(*args)
 
 
-def last_kernel(
-    tokens_grad, branch_grad, w_in_t, w_out_grad, small, gates, decay_param,
-    o_tokens, o_branch, o_w_in, o_w_out, o_conv, o_ga, o_gab, o_gi, o_gib, o_decay,
-):
-    o_tokens[...] = tokens_grad[...]
-    o_branch[...] = branch_grad[...]
-    o_w_in[...] = w_in_t[...].T
-    o_w_out[...] = w_out_grad[...]
-    o_conv[...] = small[pl.ds(0, 4), :]
-    rows = small[...]
-    o_gab[...] = rows[5]
-    o_gib[...] = rows[6]
-    o_decay[...] = rows[4] * -jax.nn.sigmoid(-decay_param[...])
-    o_ga[...] = gates[0].astype(F32)
-    o_gi[...] = gates[1].astype(F32)
+def last_kernel(*refs):
+    sems = refs[20]
+    copies = [pltpu.make_async_copy(refs[n], refs[10 + n], sems.at[n]) for n in range(10)]
+    for copy in copies:
+        copy.start()
+    for copy in copies:
+        copy.wait()
 
 
 def shards(*args):
-    results = call_first(*args)
-    S = jax.ShapeDtypeStruct
-    outs = (
-        S((32, DM), BF16),
-        S((256, CH), BF16),
-        S((128, CH), F32),
-        S((CH, 128), F32),
-        S((4, CH), F32),
-        S((2, 256, 256), F32),
-        S((CH,), F32),
-        S((2, 256, 256), F32),
-        S((CH,), F32),
-        S((CH,), F32),
-    )
     return pl.pallas_call(
         last_kernel,
-        out_shape=outs,
-        in_specs=[pl.BlockSpec(memory_space=pltpu.VMEM)] * 7,
-        out_specs=tuple(pl.BlockSpec(memory_space=pltpu.VMEM) for _ in outs),
-    )(*results, args[9])
+        out_shape=OUTS,
+        in_specs=[pl.BlockSpec(memory_space=pl.ANY)] * 10,
+        out_specs=tuple(pl.BlockSpec(memory_space=pl.ANY) for _ in OUTS),
+        scratch_shapes=[pltpu.SemaphoreType.DMA((10,))],
+    )(*call_first(*args))
 
 
 def solution(mesh):

time: 112 us -> 171 us (1.53)
  Pallas kernels: 110 us -> 170 us
    pallas_call x1, Pallas kernels: 2.77 us -> 65.2 us  [shards(): pl.pallas_call(last_kernel, out_shape=OUTS, in_specs=[pl.BlockSpec(memory...]
    pallas_call x1, Pallas kernels: 108 us -> 105 us  [call_first(): pl.pallas_call(first_kernel, out_shape=outs, in_specs=[pl.BlockSpec(memor...]
where the time goes in v4:
time: 171 us
  Pallas kernels  170 us (99%)
    pallas_call x1, Pallas kernels, call_first(): pl.pallas_call(first_kernel, out_shape=outs, in_specs=[pl.BlockSpec(memor...  105 us
    pallas_call x1, Pallas kernels, shards(): pl.pallas_call(last_kernel, out_shape=OUTS, in_specs=[pl.BlockSpec(memory...  65.2 us

profile of v4, /device:TPU:1, one launch (start us, length us, event | category | flops | bytes accessed | tf_op | source)
XLA Modules:
  0.0 171.0 jit_solution(5708196897092827343)
XLA Ops:
  0.6 105.1 %shard_map.204 = (bf16[32,4096]{1,0:T(8,128)(2,1)}, bf16[256,512]{1,0:T(8,128)(2,1)}, f32[128,512]{1,0:T(8,128)}, f32[512,128]{1,0:T(8,128)}, f32[4,512]{1,0:T(4...) custom-call(bf16[32,4096]{1,0:T(8,128)(2,1)} %tokens.1, ...), custom_call_target="tpu_custom_call" | custom-call | tf_op jit(solution)/shard_map/pallas_call | solution.py:930
  105.8 65.2 %shard_map.205 = (bf16[32,4096]{1,0:T(8,128)(2,1)}, bf16[256,512]{1,0:T(8,128)(2,1)}, f32[128,512]{1,0:T(8,128)}, f32[512,128]{1,0:T(8,128)}, f32[4,512]{1,0:T(4...) custom-call(bf16[32,4096]{1,0:T(8,128)(2,1)} %get-tuple-element.20.refs_0_, ...), custom_call_target="tpu_custom_call" | custom-call | tf_op jit(solution)/shard_map/pallas_call | solution.py:1018

commit v5 on v4

--- a/solution.py
+++ b/solution.py
@@ -558,7 +558,6 @@
     br[...] = to_segments(branch_v[...].astype(F32))
 
     tokens_in.arrive(0)
-    grads_in.send(0)
     for load in loads[3:]:
         load.wait()
     tokens_in.arrive(1)
@@ -572,7 +571,7 @@
     lax.fori_loop(0, 4, turn_weights, 0)
     tokens_in.arrive(2)
     lax.fori_loop(4, 8, turn_weights, 0)
-    grads_in.arrive(0)
+    grads_in.send(0)
     tokens_in.arrive(3)
     other_tokens = CoreColumns(p, tok, tok_o, ps.at[0], pr.at[0])
     other_grads = CoreColumns(p, og, og_o, ps.at[1], pr.at[1])
@@ -607,6 +606,7 @@
     edge_s[...] = acc[pl.ds(240, 16), :].astype(BF16)
     forward_edge = remote(edge_s, edge_r, es.at[0], er.at[0], p.along_ctx(1))
     forward_edge.start()
+    grads_in.arrive(0)
     px[pl.ds(3, 32)] = to_segments(acc[...].astype(BF16).astype(F32))
 
     lane8 = lax.broadcasted_iota(jnp.int32, (8, CH), 0)
@@ -617,6 +617,8 @@
     for j in range(3):
         turned = pltpu.roll(px[32 + j], 1, 0)
         px[j] = jnp.where(lane8 == 0, wide(before[j : j + 1]), turned)
+
+    grads_in.arrive(1)
 
     def convolve(n, carry):
         total = kv[0] * px[pl.ds(2 * n + 3, 2)]
@@ -670,13 +672,46 @@
     h_before = jnp.where(lane8 == 0, 0.0, pltpu.roll(h, 1, 0))
     states = Everyone(p, all_s, fs, fr)
     states.start(jnp.concatenate([c[7:8], h[7:8]], 0))
-    grads_in.arrive(1)
 
     def suffix(n, e):
         ep[31 - n] = e
         return e * dk[31 - n]
 
     lax.fori_loop(0, 32, suffix, jnp.ones((8, CH), F32))
+    def coefficients(n, carry):
+        at = pl.ds(2 * n, 2)
+        decay, remain, inp, recur, wide_conv = dk[at], rem[at], ig[at], rg[at], cv[at]
+        scaler = jnp.sqrt(remain)
+        inner = inp * wide_conv
+        cg[at] = 2.0 * decay * decay * inner / jnp.sqrt(jnp.maximum(4.0 * remain, 1e-06))
+        rem[at] = scaler * inp
+        ig[at] = inner * scaler * (1.0 - inp)
+        rg[at] = -8.0 * recur
+        cv[at] = kv[6] * (1.0 - recur)
+        return carry
+
+    lax.fori_loop(0, 16, coefficients, 0)
+    grads_in.arrive(2)
+    there = (0, 1, 7, 2, 6, 3, 5)
+
+    def place_of(offset):
+        return lax.rem(p.m + offset, NMP)
+
+    def early_product(n, carry):
+        at = pl.ds(pl.multiple_of(n * 1024, 1024), 1024)
+        rows = jnp.concatenate([og[place_of(o), :, at] for o in there], 0)
+        value = jnp.dot(rows, w_out_t[at, :], preferred_element_type=F32).reshape(7, 32, CH)
+        pieces[pl.ds(0, 7)] = jnp.where(n == 0, value, pieces[pl.ds(0, 7)] + value)
+        return carry
+
+    def late_product(n, carry):
+        at = pl.ds(pl.multiple_of(n * 1024, 1024), 1024)
+        return carry + jnp.dot(og[place_of(4), :, at], w_out_t[at, :], preferred_element_type=F32)
+
+    pieces[...] = jnp.zeros_like(pieces)
+    lax.fori_loop(0, 4, early_product, 0)
+    for n, offset in enumerate(there):
+        acc[pl.ds(pl.multiple_of(place_of(offset) * 32, 32), 32), :] = pieces[n]
     states.finish()
     state = state_init[...].reshape(1, CH)
     for o in range(32):
@@ -691,6 +726,9 @@
         value = hs[pl.ds(2 * n + 1, 2)] + cp[at] * seg_state
         hs[pl.ds(2 * n + 1, 2)] = value
         cp[at] = value * br[at]
+        rate_part = rg[at] * (hs[at] * dk[at] - cg[at])
+        rg[at] = rate_part
+        cv[at] = rate_part * cv[at]
         return carry
 
     lax.fori_loop(0, 16, finish_states, 0)
@@ -698,43 +736,6 @@
     lhs_g[0] = gated[...].T
     other_gated.start()
 
-    def coefficients(n, carry):
-        at = pl.ds(2 * n, 2)
-        decay, remain, inp, recur, wide_conv = dk[at], rem[at], ig[at], rg[at], cv[at]
-        scaler = jnp.sqrt(remain)
-        inner = inp * wide_conv
-        log_part = hs[at] * decay - 2.0 * decay * decay * inner / jnp.sqrt(
-            jnp.maximum(4.0 * remain, 1e-06)
-        )
-        rate_part = -8.0 * recur * log_part
-        rem[at] = scaler * inp
-        ig[at] = inner * scaler * (1.0 - inp)
-        rg[at] = rate_part
-        cv[at] = rate_part * kv[6] * (1.0 - recur)
-        return carry
-
-    lax.fori_loop(0, 16, coefficients, 0)
-    grads_in.arrive(2)
-    there = (0, 1, 7, 2, 6, 3, 5)
-
-    def place_of(offset):
-        return lax.rem(p.m + offset, NMP)
-
-    def early_product(n, carry):
-        at = pl.ds(pl.multiple_of(n * 1024, 1024), 1024)
-        rows = jnp.concatenate([og[place_of(o), :, at] for o in there], 0)
-        value = jnp.dot(rows, w_out_t[at, :], preferred_element_type=F32).reshape(7, 32, CH)
-        pieces[pl.ds(0, 7)] = jnp.where(n == 0, value, pieces[pl.ds(0, 7)] + value)
-        return carry
-
-    def late_product(n, carry):
-        at = pl.ds(pl.multiple_of(n * 1024, 1024), 1024)
-        return carry + jnp.dot(og[place_of(4), :, at], w_out_t[at, :], preferred_element_type=F32)
-
-    pieces[...] = jnp.zeros_like(pieces)
-    lax.fori_loop(0, 4, early_product, 0)
-    for n, offset in enumerate(there):
-        acc[pl.ds(pl.multiple_of(place_of(offset) * 32, 32), 32), :] = pieces[n]
     grads_in.arrive(3)
     other_grads.start()
     acc[pl.ds(pl.multiple_of(place_of(4) * 32, 32), 32), :] = lax.fori_loop(
@@ -1006,11 +1007,15 @@
 
 
 def last_kernel(*refs):
-    sems = refs[20]
-    copies = [pltpu.make_async_copy(refs[n], refs[10 + n], sems.at[n]) for n in range(10)]
-    for copy in copies:
+    given, results, held, sems = refs[:10], refs[10:20], refs[20:30], refs[30]
+    into = [pltpu.make_async_copy(given[n], held[n], sems.at[0, n]) for n in range(10)]
+    out = [pltpu.make_async_copy(held[n], results[n], sems.at[1, n]) for n in range(10)]
+    for copy in into:
         copy.start()
-    for copy in copies:
+    for n in range(10):
+        into[n].wait()
+        out[n].start()
+    for copy in out:
         copy.wait()
 
 
@@ -1020,7 +1025,8 @@
         out_shape=OUTS,
         in_specs=[pl.BlockSpec(memory_space=pl.ANY)] * 10,
         out_specs=tuple(pl.BlockSpec(memory_space=pl.ANY) for _ in OUTS),
-        scratch_shapes=[pltpu.SemaphoreType.DMA((10,))],
+        scratch_shapes=[pltpu.VMEM(one.shape, one.dtype) for one in OUTS]
+        + [pltpu.SemaphoreType.DMA((2, 10))],
     )(*call_first(*args))
 
 

time: 171 us -> 104 us (0.61)
  Pallas kernels: 170 us -> 104 us
    pallas_call x1, Pallas kernels: 65.2 us -> 2.53 us  [shards(): pl.pallas_call(last_kernel, out_shape=OUTS, in_specs=[pl.BlockSpec(memory...]
    pallas_call x1, Pallas kernels: 105 us -> 101 us  [call_first(): pl.pallas_call(first_kernel, out_shape=outs, in_specs=[pl.BlockSpec(memor...]
where the time goes in v5:
time: 104 us
  Pallas kernels  104 us (100%)
    pallas_call x1, Pallas kernels, call_first(): pl.pallas_call(first_kernel, out_shape=outs, in_specs=[pl.BlockSpec(memor...  101 us
    pallas_call x1, Pallas kernels, shards(): pl.pallas_call(last_kernel, out_shape=OUTS, in_specs=[pl.BlockSpec(memory...  2.53 us

profile of v5, /device:TPU:1, one launch (start us, length us, event | category | flops | bytes accessed | tf_op | source)
XLA Modules:
  0.0 104.2 jit_solution(7807870999102512252)
XLA Ops:
  0.6 101.1 %shard_map.204 = (bf16[32,4096]{1,0:T(8,128)(2,1)}, bf16[256,512]{1,0:T(8,128)(2,1)}, f32[128,512]{1,0:T(8,128)}, f32[512,128]{1,0:T(8,128)}, f32[4,512]{1,0:T(4...) custom-call(bf16[32,4096]{1,0:T(8,128)(2,1)} %tokens.1, ...), custom_call_target="tpu_custom_call" | custom-call | tf_op jit(solution)/shard_map/pallas_call | solution.py:931
  101.7 2.5 %shard_map.205 = (bf16[32,4096]{1,0:T(8,128)(2,1)}, bf16[256,512]{1,0:T(8,128)(2,1)}, f32[128,512]{1,0:T(8,128)}, f32[512,128]{1,0:T(8,128)}, f32[4,512]{1,0:T(4...) custom-call(bf16[32,4096]{1,0:T(8,128)(2,1)} %get-tuple-element.20.refs_0_, ...), custom_call_target="tpu_custom_call" | custom-call | tf_op jit(solution)/shard_map/pallas_call | solution.py:1023

commit v6 on v5

--- a/solution.py
+++ b/solution.py
@@ -570,8 +570,8 @@
 
     lax.fori_loop(0, 4, turn_weights, 0)
     tokens_in.arrive(2)
+    grads_in.send(0)
     lax.fori_loop(4, 8, turn_weights, 0)
-    grads_in.send(0)
     tokens_in.arrive(3)
     other_tokens = CoreColumns(p, tok, tok_o, ps.at[0], pr.at[0])
     other_grads = CoreColumns(p, og, og_o, ps.at[1], pr.at[1])
@@ -618,8 +618,6 @@
         turned = pltpu.roll(px[32 + j], 1, 0)
         px[j] = jnp.where(lane8 == 0, wide(before[j : j + 1]), turned)
 
-    grads_in.arrive(1)
-
     def convolve(n, carry):
         total = kv[0] * px[pl.ds(2 * n + 3, 2)]
         for j in (1, 2, 3):
@@ -678,6 +676,8 @@
         return e * dk[31 - n]
 
     lax.fori_loop(0, 32, suffix, jnp.ones((8, CH), F32))
+    grads_in.arrive(1)
+
     def coefficients(n, carry):
         at = pl.ds(2 * n, 2)
         decay, remain, inp, recur, wide_conv = dk[at], rem[at], ig[at], rg[at], cv[at]
@@ -792,18 +792,23 @@
         )
 
     zero = jnp.zeros((8, CH), F32)
-    sum_a, sum_i, sum_r = lax.fori_loop(0, 16, gate_grads, (zero, zero, zero))
-    other_gate.start()
-    for b in (0, 1):
-        cols = pl.ds(b * 256, 256)
-        cg[pl.ds(0, 32), :, cols] += (
-            matmul_nt(ri[0, :, cols], gate_a[b]) + matmul_nt(ri[1, :, cols], gate_i[b])
-        ).reshape(32, 8, 256)
+    def through_gates(low, high):
+        rows = pl.ds(low * 8, (high - low) * 8)
+        for b in (0, 1):
+            cols = pl.ds(b * 256, 256)
+            cg[pl.ds(low, high - low), :, cols] += (
+                matmul_nt(ri[0, rows, cols], gate_a[b]) + matmul_nt(ri[1, rows, cols], gate_i[b])
+            ).reshape(high - low, 8, 256)
+
+    first_sums = lax.fori_loop(0, 2, gate_grads, (zero, zero, zero))
+    through_gates(0, 4)
     backward_edge = remote(cg.at[pl.ds(0, 3)], edge_c, es.at[1], er.at[1], p.along_ctx(31))
     backward_edge.start()
+    sum_a, sum_i, sum_r = lax.fori_loop(2, 16, gate_grads, first_sums)
+    other_gate.start()
+    through_gates(4, 32)
     w_out_sum.joined()
     w_out_sum.others()
-    w_out_sum.keep()
     backward_edge.wait_recv()
     for j in range(3):
         turned = pltpu.roll(cg[j], 7, 0)
@@ -835,36 +840,39 @@
 
         lax.fori_loop(part * 4, part * 4 + 4, spread, 0)
         row_sum.begin(part)
+        if part == 0:
+            other_conv.finish()
+            other_gate.finish()
+            for b in (0, 1):
+                cols = pl.ds(b * 256, 256)
+                gate_p[b] = (
+                    matmul_tn(conv_b[:, cols], ri[p.k, :, cols])
+                    + matmul_tn(conv_o[:, cols], ri_o[:, cols])
+                ).astype(BF16)
+            gate_sum.start(0)
     rows = [jnp.sum(v, 0, keepdims=True) for v in (*tap_sums, sum_r, sum_a, sum_i)]
     total_sum.start(0, jnp.concatenate(rows + [jnp.zeros((1, CH), F32)], 0))
-    other_conv.finish()
-    other_gate.finish()
-    for b in (0, 1):
-        cols = pl.ds(b * 256, 256)
-        gate_p[b] = (
-            matmul_tn(conv_b[:, cols], ri[p.k, :, cols]) + matmul_tn(conv_o[:, cols], ri_o[:, cols])
-        ).astype(BF16)
-    gate_sum.start(0)
     other_tokens.finish()
     other_proj.finish()
     w_in_sum.relay()
     w_in_sum.fresh()
     row_sum.step(1)
+    w_out_sum.keep()
     w_out_sum.turn()
     w_in_sum.joined()
     w_in_sum.others()
-    row_sum.step(2)
-    w_in_sum.keep()
     gate_sum.finish(0)
     gate_sum.start(1)
-    w_out_sum.join()
+    row_sum.step(2)
     total_sum.finish(0)
     total_sum.start(1, core_m[0] + core_m[1])
+    w_in_sum.keep()
     w_in_sum.turn()
+    w_out_sum.join()
     row_sum.step(3)
-    w_in_sum.join()
     gate_sum.finish(1)
     gate_sum.start(2)
+    w_in_sum.join()
     total_sum.finish(1)
     total_sum.start(2, row_m[0] + row_m[1] + row_m[2] + row_m[3])
     gates_out = (gate_a_grad, gate_i_grad)
@@ -876,10 +884,10 @@
     bias_a_grad[...] = small[5]
     bias_i_grad[...] = small[6]
     decay_grad[...] = small[4] * -jax.nn.sigmoid(-decay_param[...])
-    row_sum.finish(tokens_grad)
     gate_sum.finish(2)
     for n in (0, 1):
         gates_out[n][...] = gate_total[n].astype(F32)
+    row_sum.finish(tokens_grad)
     for used in (states, adjoints, total_sum, w_out_sum, w_in_sum, row_sum, gate_sum, *pairs):
         used.drain()
     tokens_in.sent()

time: 104 us -> 102 us (0.981)
  Pallas kernels: 104 us -> 102 us
    pallas_call x1, Pallas kernels: 101 us -> 99 us  [call_first(): pl.pallas_call(first_kernel, out_shape=outs, in_specs=[pl.BlockSpec(memor...]
where the time goes in v6:
time: 102 us
  Pallas kernels  102 us (100%)
    pallas_call x1, Pallas kernels, call_first(): pl.pallas_call(first_kernel, out_shape=outs, in_specs=[pl.BlockSpec(memor...  99 us
    pallas_call x1, Pallas kernels, shards(): pl.pallas_call(last_kernel, out_shape=OUTS, in_specs=[pl.BlockSpec(memory...  2.53 us

profile of v6, /device:TPU:1, one launch (start us, length us, event | category | flops | bytes accessed | tf_op | source)
XLA Modules:
  0.0 102.2 jit_solution(370469320797401160)
XLA Ops:
  0.6 99.0 %shard_map.204 = (bf16[32,4096]{1,0:T(8,128)(2,1)}, bf16[256,512]{1,0:T(8,128)(2,1)}, f32[128,512]{1,0:T(8,128)}, f32[512,128]{1,0:T(8,128)}, f32[4,512]{1,0:T(4...) custom-call(bf16[32,4096]{1,0:T(8,128)(2,1)} %tokens.1, ...), custom_call_target="tpu_custom_call" | custom-call | tf_op jit(solution)/shard_map/pallas_call | solution.py:939
  99.7 2.5 %shard_map.205 = (bf16[32,4096]{1,0:T(8,128)(2,1)}, bf16[256,512]{1,0:T(8,128)(2,1)}, f32[128,512]{1,0:T(8,128)}, f32[512,128]{1,0:T(8,128)}, f32[4,512]{1,0:T(4...) custom-call(bf16[32,4096]{1,0:T(8,128)(2,1)} %get-tuple-element.20.refs_0_, ...), custom_call_target="tpu_custom_call" | custom-call | tf_op jit(solution)/shard_map/pallas_call | solution.py:1031

commit v7 on v6

--- a/solution.py
+++ b/solution.py
@@ -568,10 +568,9 @@
         w_in_t[:, at] = w_in_v[at, :].T
         return carry
 
-    lax.fori_loop(0, 4, turn_weights, 0)
     tokens_in.arrive(2)
     grads_in.send(0)
-    lax.fori_loop(4, 8, turn_weights, 0)
+    lax.fori_loop(0, 8, turn_weights, 0)
     tokens_in.arrive(3)
     other_tokens = CoreColumns(p, tok, tok_o, ps.at[0], pr.at[0])
     other_grads = CoreColumns(p, og, og_o, ps.at[1], pr.at[1])

time: 102 us -> 102 us (level)
  no operation moved by 1% of the time
where the time goes in v7:
time: 102 us
  Pallas kernels  102 us (100%)
    pallas_call x1, Pallas kernels, call_first(): pl.pallas_call(first_kernel, out_shape=outs, in_specs=[pl.BlockSpec(memor...  99 us
    pallas_call x1, Pallas kernels, shards(): pl.pallas_call(last_kernel, out_shape=OUTS, in_specs=[pl.BlockSpec(memory...  2.53 us

profile of v7, /device:TPU:1, one launch (start us, length us, event | category | flops | bytes accessed | tf_op | source)
XLA Modules:
  0.0 102.2 jit_solution(14513326354733367480)
XLA Ops:
  0.6 99.0 %shard_map.204 = (bf16[32,4096]{1,0:T(8,128)(2,1)}, bf16[256,512]{1,0:T(8,128)(2,1)}, f32[128,512]{1,0:T(8,128)}, f32[512,128]{1,0:T(8,128)}, f32[4,512]{1,0:T(4...) custom-call(bf16[32,4096]{1,0:T(8,128)(2,1)} %tokens.1, ...), custom_call_target="tpu_custom_call" | custom-call | tf_op jit(solution)/shard_map/pallas_call | solution.py:938
  99.7 2.5 %shard_map.205 = (bf16[32,4096]{1,0:T(8,128)(2,1)}, bf16[256,512]{1,0:T(8,128)(2,1)}, f32[128,512]{1,0:T(8,128)}, f32[512,128]{1,0:T(8,128)}, f32[4,512]{1,0:T(4...) custom-call(bf16[32,4096]{1,0:T(8,128)(2,1)} %get-tuple-element.20.refs_0_, ...), custom_call_target="tpu_custom_call" | custom-call | tf_op jit(solution)/shard_map/pallas_call | solution.py:1030
